TPU v7x, 512 devices: a whole 4x4x16 slice. The times are simulated.
512 devices in a mesh: rows: 64 (over z_hi, y, x, core), slab: 8 (over z_lo).
Axes of the slice: x: 4, y: 4, z: 16 (z_hi: 2, z_lo: 8; z = z_hi * 8 + z_lo), core: 2. Of those that a mesh axis runs over, the one named last changes fastest.
Arguments:
- prior_vectors: float32 [458752, 384], P(('rows', 'slab'))
- raw_columns: float32 [2, 458752, 256], P(None, ('rows', 'slab')), as said below
- pivot_rows: int32 [2, 256], replicated, may hold values from 0 to 458751, as said below
Outputs:
- new_vectors: float32 [2, 458752, 256], P(None, ('rows', 'slab'))
Inputs may be any that keep to these rules, and one draw needn't show every extreme that they name: `pivot_rows`: all 512 entries are distinct pair rows. `raw_columns`: in every step the matrix symmetric of the steps is positive definite.
All inputs are finite; a program needn't handle non-finite values.
Results may differ from a plain program's by a relative error of at most 0.0001.
Values sent between devices are 32-bit elements; how exact they have to be, the bound alone decides.
No kernel may reach another device: no remote copies, remote signals or barrier semaphores. Data moves between devices by JAX's collectives and lax.ppermute only.
A program may use at most 64 MiB of HBM per device.

v0:
```python
import jax
import jax.numpy as jnp
from jax import lax
from jax.sharding import PartitionSpec as P


def pivot_sum(portion):
    return lax.psum(portion, ("rows", "slab"))


def body(prior_vectors, raw_columns, pivot_rows):
    highest = lax.Precision.HIGHEST
    rows_here = prior_vectors.shape[0]
    pivot_count = raw_columns.shape[2]
    step_count = raw_columns.shape[0]
    offset = lax.axis_index(("rows", "slab")) * rows_here
    positions = jnp.arange(rows_here, dtype=jnp.int32)
    selectors = []
    for which_step in range(step_count):
        local_index = pivot_rows[which_step] - offset
        selectors.append((local_index[:, None] == positions[None, :]).astype(jnp.float32))
    vectors = prior_vectors
    outputs = []
    for which_step in range(step_count):
        joined = jnp.concatenate([vectors, raw_columns[which_step]], axis=1)
        summed = pivot_sum(jnp.dot(selectors[which_step], joined, precision=highest))
        pivot_vec = summed[:, : vectors.shape[1]]
        pivot_raw = summed[:, vectors.shape[1] :]
        residual = raw_columns[which_step] - jnp.dot(vectors, pivot_vec.T, precision=highest)
        pivot_block = pivot_raw - jnp.dot(pivot_vec, pivot_vec.T, precision=highest)
        symmetric = 0.5 * (pivot_block + pivot_block.T)
        factor = jnp.linalg.cholesky(symmetric)
        identity = jnp.eye(pivot_count, dtype=jnp.float32)
        inverse = lax.linalg.triangular_solve(factor, identity, left_side=True, lower=True)
        fresh_vec = jnp.dot(residual, inverse.T, precision=highest)
        outputs.append(fresh_vec)
        vectors = jnp.concatenate([vectors, fresh_vec], axis=1)
    return jnp.stack(outputs)


def solution(mesh):
    return jax.shard_map(
        body,
        mesh=mesh,
        in_specs=(P(("rows", "slab"), None), P(None, ("rows", "slab"), None), P()),
        out_specs=P(None, ("rows", "slab"), None),
        check_vma=False,
    )
```

profile of v0, /device:TPU:1, one launch (start us, length us, event | category | flops | bytes accessed | tf_op | source)
XLA Modules:
  0.0 1130.4 jit_solution(11523989284678516976)
XLA Ops:
  6.5 2.6 slice_bitcast_fusion
  9.2 2.5 fusion.6
  11.8 469.7 %all-reduce.4.cloned.1.call-done = f32[256,640]{1,0:T(8,128)} async-done(((f32[256,640]{1,0:T(8,128)}), f32[256,640]{1,0:T(8,128)}) %all-reduce.4.cloned.1.call-update) | async-done | bytes 655376 | tf_op jit(solution)/shard_map/psum | solution.py:8
  481.5 1.8 convolution_subtract_fusion
  483.6 0.7 copy-done.5
  484.3 11.7 %cholesky.130 = f32[128,128]{1,0:T(8,128)S(1)} custom-call(f32[128,128]{1,0:T(8,128)S(1)} %cholesky.194), custom_call_target="Cholesky" | custom-call | tf_op jit(solution)/shard_map/jit(cholesky)/cholesky | solution.py:32
  496.7 11.4 %custom-call.13 = f32[1,128,128]{1,2,0:T(8,128)} custom-call(f32[1,128,128]{2,1,0:T(8,128)} %get-tuple-element.52), custom_call_target="InvertDiagBlocksLowerTriangular" | custom-call | tf_op jit(solution)/shard_map/jit(cholesky)/cholesky | solution.py:32
  508.1 0.7 cholesky.155
  508.8 1.7 constant_dynamic-update-slice_fusion.3
  510.5 1.7 convolution_subtract_fusion.5
  512.2 12.5 %cholesky.147 = f32[128,128]{1,0:T(8,128)S(1)} custom-call(f32[128,128]{1,0:T(8,128)} %convolution_subtract_fusion.5), custom_call_target="Cholesky" | custom-call | tf_op jit(solution)/shard_map/jit(cholesky)/cholesky | solution.py:32
  525.4 0.7 compare_reduce_fusion.2
  527.3 1.7 select_select_fusion.1
  529.8 7.4 while.4
  530.8 2.9 bitcast_dynamic-update-slice_fusion.4
  534.3 2.8 bitcast_dynamic-update-slice_fusion.4
  537.1 21.1 %custom-call.14 = f32[2,128,128]{1,2,0:T(8,128)} custom-call(f32[2,128,128]{2,1,0:T(8,128)} %get-tuple-element.21), custom_call_target="InvertDiagBlocksLowerTriangular" | custom-call | tf_op jit(solution)/shard_map/triangular_solve/custom-call.0 | solution.py:34
  558.2 1.1 fusion.32
  559.4 1.1 convolution_subtract_fusion.3
  560.5 1.1 fusion.39
  561.7 2.6 fusion.11
  564.3 1.1 fusion.18
  565.6 4.2 fusion
  569.9 458.7 %all-reduce.6.cloned.1.call-done = f32[256,896]{1,0:T(8,128)} async-done(((f32[256,896]{1,0:T(8,128)}), f32[256,896]{1,0:T(8,128)}) %all-reduce.6.cloned.1.call-update) | async-done | bytes 917520 | tf_op jit(solution)/shard_map/psum | solution.py:8
  1028.6 2.2 convolution_subtract_fusion.1
  1031.5 0.8 copy.8
  1032.3 1.1 fusion.26
  1033.4 0.8 copy.9
  1034.2 1.0 fusion.25
  1036.6 12.5 %cholesky.164 = f32[128,128]{1,0:T(8,128)S(1)} custom-call(f32[128,128]{1,0:T(8,128)} %cholesky.197), custom_call_target="Cholesky" | custom-call | tf_op jit(solution)/shard_map/jit(cholesky)/cholesky | solution.py:32
  1049.8 0.7 cholesky.189
  1050.5 10.8 custom-call.15
  1061.3 1.7 constant_dynamic-update-slice_fusion.1
  1062.9 1.7 convolution_subtract_fusion.4
  1064.7 12.5 %cholesky.181 = f32[128,128]{1,0:T(8,128)S(1)} custom-call(f32[128,128]{1,0:T(8,128)} %convolution_subtract_fusion.4), custom_call_target="Cholesky" | custom-call | tf_op jit(solution)/shard_map/jit(cholesky)/cholesky | solution.py:32
  1077.9 0.7 compare_reduce_fusion
  1080.5 1.7 select_select_fusion
  1082.9 7.0 while.5
  1083.5 2.9 bitcast_dynamic-update-slice_fusion.5
  1087.1 2.8 bitcast_dynamic-update-slice_fusion.5
  1089.9 21.1 %custom-call.16 = f32[2,128,128]{1,2,0:T(8,128)} custom-call(f32[2,128,128]{2,1,0:T(8,128)} %get-tuple-element.22), custom_call_target="InvertDiagBlocksLowerTriangular" | custom-call | tf_op jit(solution)/shard_map/triangular_solve/custom-call.0 | solution.py:34
  1111.0 1.1 fusion.30
  1112.1 1.1 convolution_subtract_fusion.2
  1113.3 1.1 fusion.35
  1114.4 3.7 fusion.10
  1118.2 1.1 convolution_bitcast_fusion
  1119.2 1.4 pad_maximum_fusion.4
  1120.6 2.7 copy.11
  (45 shorter events, 10.1 us)
Async XLA Ops:
  6.5 474.9 %all-reduce.4.cloned.1.call-start = ((), (), s32[]{:S(2)}) async-start(), calls=%async_computation | async-start | bytes 1310720 | tf_op jit(solution)/shard_map/psum | solution.py:8
  6.5 2.6 copy-start.7
  6.5 2.6 copy-start
  11.7 1017.0 %all-reduce.6.cloned.1.call-start = ((), (), s32[]{:S(2)}) async-start(), calls=%async_computation.1 | async-start | bytes 1835008 | tf_op jit(solution)/shard_map/psum | solution.py:8
  11.7 547.6 %copy-start.3 = (f32[256,256]{1,0:T(8,128)}, f32[256,256]{1,0:T(8,128)S(1)}, u32[]{:S(2)}) copy-start(f32[256,256]{1,0:T(8,128)S(1)} %fusion.29) | copy-start | bytes 786436
  483.6 0.7 copy-start.5
  496.7 65.0 %copy-start.1 = (f32[2,896,256]{2,1,0:T(8,128)S(1)}, f32[2,896,256]{2,1,0:T(8,128)}, u32[]{:S(2)}) copy-start(f32[2,896,256]{2,1,0:T(8,128)} %param.7) | copy-start | bytes 5505028
  1030.8 0.7 copy-start.2
  1035.2 0.7 copy-start.6
  1035.9 75.1 %copy-start.4 = (f32[256,256]{1,0:T(8,128)S(1)}, f32[256,256]{1,0:T(8,128)}, u32[]{:S(2)}) copy-start(f32[256,256]{1,0:T(8,128)} %copy-done.3) | copy-start | bytes 786436
Sparse Core Ops, SparseCore 0:
  12.8 468.5 all-reduce.3
  570.0 458.5 all-reduce.5
where the time goes:
time: 1150 us; the launch traced here: 1130 us
  waiting for transfers between devices  928 us (81%)
  other arithmetic  125 us (11%)
  matrix products  32.8 us (3%)
  local copies, waits for them, and re-layouts  27.2 us (2%)
  between operations  16.4 us (1%)
    psum x2, waiting for transfers between devices, pivot_sum(): return lax.psum(portion, ('rows', 'slab'))  928 us
    another operation x13, other arithmetic, body(): factor = jnp.linalg.cholesky(symmetric)  76.1 us
    another operation x5, other arithmetic, body(): lax.linalg.triangular_solve(factor, identity, left_side=True, lower=True)  45.6 us
  transfers between devices with their start and end apart: 2, of which 2 were waited for; matrix products, arithmetic and copies ran while one was open for 0% of the time, Pallas kernels for 0%

commit v1 on v0

v1 whole, which is shorter than its diff:
```python
import functools

import jax
import jax.numpy as jnp
from jax import lax
from jax.experimental import pallas as pl
from jax.experimental.pallas import tpu as pltpu
from jax.sharding import Mesh
from jax.sharding import PartitionSpec as P

F32 = jnp.float32
HIGHEST = lax.Precision.HIGHEST
AXES = ("z_hi", "y", "x", "core", "z_lo")
TILE = (8, 128)
VMEM_LIMIT = 48 * 1024 * 1024


def dot(left, right, left_dim=1, right_dim=0):
    dims = (((left_dim,), (right_dim,)), ((), ()))
    return lax.dot_general(left, right, dims, precision=HIGHEST, preferred_element_type=F32)


def pack_kernel(pivots, place, prior, raw, keep, send):
    keep[...] = jnp.zeros_like(keep)
    send[...] = jnp.zeros_like(send)
    offset, core = place[0], place[1]
    rows_here = prior.shape[0]
    groups = keep.shape[0]
    half = groups * 8

    for step in range(2):
        base = 5 * step

        def look(pivot, step=step, base=base):
            row = pivots[step, pivot] - offset
            here = jnp.logical_and(row >= 0, row < rows_here)

            @pl.when(here)
            def _():
                side = pivot // half
                group = lax.rem(pivot, half) // 8
                line = pl.ds(lax.rem(pivot, 8), 1)

                def put(target):
                    values = prior[pl.ds(row, 1), :]
                    for t in range(3):
                        target[group, base + t, line, :] = values[:, 128 * t : 128 * t + 128]
                    for which in range(step + 1):
                        values = raw[which, pl.ds(row, 1), :]
                        for t in range(2):
                            target[group, base + 3 + 2 * which + t, line, :] = values[:, 128 * t : 128 * t + 128]

                @pl.when(side == core)
                def _():
                    put(keep)

                @pl.when(side != core)
                def _():
                    put(send)

        def chunk(which, _):
            for k in range(8):
                look(which * 8 + k)
            return 0

        lax.fori_loop(0, pivots.shape[1] // 8, chunk, 0)


def pack(pivot_rows, place, prior, raw, groups):
    shape = jax.ShapeDtypeStruct((groups, 12) + TILE, F32)
    vmem, smem = pl.BlockSpec(memory_space=pltpu.VMEM), pl.BlockSpec(memory_space=pltpu.SMEM)
    return pl.pallas_call(
        pack_kernel,
        out_shape=(shape, shape),
        in_specs=[smem, smem, vmem, vmem],
        out_specs=(vmem, vmem),
        compiler_params=pltpu.CompilerParams(vmem_limit_bytes=VMEM_LIMIT),
    )(pivot_rows, place, prior, raw)


def eliminate(block, panel):
    width = block.shape[0]
    lanes = 2 * width
    row_of = lax.broadcasted_iota(jnp.int32, (width, width), 0)
    column_of = lax.broadcasted_iota(jnp.int32, (width, width), 1)
    work = jnp.concatenate([block, (row_of == column_of).astype(F32)], axis=1)
    done = []
    for first in range(0, width, panel):
        left = width - first
        columns = [jnp.broadcast_to(work[:, first + k : first + k + 1], (left, lanes)) for k in range(panel)]
        rows, scaled = [], []
        for k in range(panel):
            pivot = jnp.broadcast_to(columns[k][k : k + 1], TILE)
            root = lax.rsqrt(pivot)
            root = (root * (1.5 - 0.5 * pivot * root * root))[0:1]
            row = work[k : k + 1]
            for before in range(k):
                row = row - scaled[before][k : k + 1] * rows[before]
            rows.append(row * root)
            scaled.append(columns[k] * root)
            for after in range(k + 1, panel):
                columns[after] = columns[after] - scaled[k] * (columns[after][k : k + 1] * root)
        done.extend(rows)
        if left > panel:
            work = work[panel:]
            for k in range(panel):
                work = work - scaled[k][panel:] * rows[k]
    return jnp.concatenate(done, axis=0)[:, width:]


def cholesky_inverse(symmetric, width=64, panel=16):
    size = symmetric.shape[0]
    work = symmetric
    finished = []
    for which in range(size // width):
        low = which * width
        rest = size - low - width
        line = work[:width]
        inverse = eliminate(line[:, low : low + width], panel)
        parts = [inverse]
        if low:
            parts.insert(0, jnp.zeros((width, low), F32))
        if rest:
            parts.append(jnp.zeros((width, rest), F32))
        block_of = lax.broadcasted_iota(jnp.int32, (width, size), 1) // width
        line = jnp.where(block_of == which, jnp.concatenate(parts, axis=1), dot(inverse, line))
        finished.append(jnp.where(block_of <= which, line, 0.0))
        if rest:
            block_of = lax.broadcasted_iota(jnp.int32, (rest, size), 1) // width
            work = jnp.where(block_of == which, 0.0, work[width:]) - dot(line[:, low + width :], line, 0, 0)
    return jnp.concatenate(finished, axis=0)


def steps_kernel(place, mine, other, prior, raw, out, packed):
    core = place[1]
    half = mine.shape[0]
    packed[pl.ds(core * half, half)] = mine[...]
    packed[pl.ds((1 - core) * half, half)] = other[...]

    def columns(first, count):
        tiles = [packed[:, first + t].reshape(2 * half * 8, 128) for t in range(count)]
        return jnp.concatenate(tiles, axis=1)

    prior_0, prior_1 = columns(0, 3), columns(5, 3)
    vectors = prior[...]

    def symmetrized(block):
        return 0.5 * (block + block.T)

    inverse_0 = cholesky_inverse(symmetrized(columns(3, 2) - dot(prior_0, prior_0, 1, 1)))
    fresh_pivots = dot(columns(8, 2) - dot(prior_1, prior_0, 1, 1), inverse_0, 1, 1)
    block_1 = columns(10, 2) - dot(prior_1, prior_1, 1, 1) - dot(fresh_pivots, fresh_pivots, 1, 1)
    inverse_1 = cholesky_inverse(symmetrized(block_1))
    fresh = dot(raw[0] - dot(vectors, prior_0, 1, 1), inverse_0, 1, 1)
    out[0] = fresh
    residual = raw[1] - dot(vectors, prior_1, 1, 1) - dot(fresh, fresh_pivots, 1, 1)
    out[1] = dot(residual, inverse_1, 1, 1)


def steps(place, mine, other, prior, raw):
    vmem, smem = pl.BlockSpec(memory_space=pltpu.VMEM), pl.BlockSpec(memory_space=pltpu.SMEM)
    groups = mine.shape[0]
    return pl.pallas_call(
        steps_kernel,
        out_shape=jax.ShapeDtypeStruct(raw.shape, F32),
        in_specs=[smem, vmem, vmem, vmem, vmem],
        out_specs=vmem,
        scratch_shapes=[pltpu.VMEM((2 * groups, 12) + TILE, F32)],
        compiler_params=pltpu.CompilerParams(vmem_limit_bytes=VMEM_LIMIT),
    )(place, mine, other, prior, raw)


def body(prior, raw, pivot_rows):
    rows_here = prior.shape[0]
    core = lax.axis_index("core")
    place = jnp.stack([lax.axis_index(AXES) * rows_here, core]).astype(jnp.int32)
    plane, line = ("y", "x"), ("z_hi", "z_lo")
    in_plane, in_line = lax.axis_size(plane), lax.axis_size(line)
    swap = [(0, 1), (1, 0)]

    keep, send = pack(pivot_rows, place, prior, raw, in_plane)
    total = keep + lax.ppermute(send, "core", swap)
    total = jnp.sum(lax.all_to_all(total, plane, 0, 0), axis=0)
    tiles = total.shape[0]
    total = jnp.concatenate([total, jnp.zeros((in_line - tiles,) + TILE, F32)], axis=0)
    total = jnp.sum(lax.all_to_all(total, line, 0, 0), axis=0)
    total = lax.all_to_all(jnp.broadcast_to(total, (in_line,) + TILE), line, 0, 0)[:tiles]
    mine = lax.all_to_all(jnp.broadcast_to(total, (in_plane,) + total.shape), plane, 0, 0)
    other = lax.ppermute(mine, "core", swap)
    return steps(place, mine, other, prior, raw)


def solution(mesh):
    fine = Mesh(mesh.devices.reshape(2, 4, 4, 2, 8), AXES)
    return jax.shard_map(
        body,
        mesh=fine,
        in_specs=(P(AXES, None), P(None, AXES, None), P()),
        out_specs=P(None, AXES, None),
        check_vma=False,
    )
```

time: 1150 us -> 131 us (0.11); the launches traced: 1130 us -> 130 us
  waiting for transfers between devices: 928 us -> 3.78 us
  other arithmetic: 125 us -> 1.52 us
  blocking collectives: 0 us -> 69.9 us
  Pallas kernels: 0 us -> 36.3 us
  matrix products: 32.8 us -> 0 us
  local copies, waits for them, and re-layouts: 27.2 us -> 3.61 us
  between operations: 16.4 us -> 0.06 us
  starting transfers between devices: 0.04 us -> 15.1 us
    psum x2 -> x0, waiting for transfers between devices: 928 us -> none  [pivot_sum(): return lax.psum(portion, ('rows', 'slab'))]
    another operation x19 -> x1, other arithmetic: 123 us -> 0.07 us  [body(): jnp.stack([lax.axis_index(AXES) * rows_here, core]).astype(jnp.int32)]
    all_to_all x0 -> x4, blocking collectives: none -> 69.9 us  [the longest x1 24 us: body(): total = jnp.sum(lax.all_to_all(total, line, 0, 0), axis=0)]
    pallas_call x0 -> x2, Pallas kernels: none -> 36.3 us  [the longest x1 29.3 us: steps(): pl.pallas_call(steps_kernel, out_shape=jax.ShapeDtypeStruct(raw.shape, F3...]
    another operation x20 -> x0, local copies, waits for them, and re-layouts: 20.3 us -> none  [the longest x15 15.5 us: body(): lax.linalg.triangular_solve(factor, identity, left_side=True, lower=True)]
    dot_general x8 -> x0, matrix products: 19.2 us -> none  [the longest x2 6.7 us: body(): jnp.dot(selectors[which_step], joined, precision=highest)]
    ppermute x0 -> x2, starting transfers between devices: none -> 15.1 us  [the longest x1 8.77 us: body(): total = keep + lax.ppermute(send, 'core', swap)]
    another operation x10 -> x0, matrix products: 13.6 us -> none  [the longest x4 6.82 us: body(): factor = jnp.linalg.cholesky(symmetric)]
where the time goes in v1:
time: 131 us; the launch traced here: 130 us
  blocking collectives  69.9 us (53%)
  Pallas kernels  36.3 us (28%)
  starting transfers between devices  15.1 us (12%)
  waiting for transfers between devices  3.78 us (3%)
  local copies, waits for them, and re-layouts  3.61 us (3%)
  other arithmetic  1.52 us (1%)
    pallas_call x1, Pallas kernels, steps(): pl.pallas_call(steps_kernel, out_shape=jax.ShapeDtypeStruct(raw.shape, F3...  29.3 us
    all_to_all x1, blocking collectives, body(): total = jnp.sum(lax.all_to_all(total, line, 0, 0), axis=0)  24 us
    all_to_all x1, blocking collectives, body(): total = jnp.sum(lax.all_to_all(total, plane, 0, 0), axis=0)  17.4 us
    all_to_all x1, blocking collectives, body(): lax.all_to_all(jnp.broadcast_to(total, (in_line,) + TILE), line, 0, 0)  14.4 us
    all_to_all x1, blocking collectives, body(): lax.all_to_all(jnp.broadcast_to(total, (in_plane,) + total.shape), plane,...  14.1 us
    ppermute x1, starting transfers between devices, body(): total = keep + lax.ppermute(send, 'core', swap)  8.77 us
    pallas_call x1, Pallas kernels, pack(): pl.pallas_call(pack_kernel, out_shape=(shape, shape), in_specs=[smem, sme...  6.98 us
    ppermute x1, starting transfers between devices, body(): other = lax.ppermute(mine, 'core', swap)  6.36 us
  transfers between devices with their start and end apart: 2, of which 2 were waited for; matrix products, arithmetic and copies ran while one was open for 0% of the time, Pallas kernels for 0%

profile of v1, /device:TPU:1, one launch (start us, length us, event | category | flops | bytes accessed | tf_op | source)
XLA Modules:
  0.0 130.3 jit_solution(10708919771546806133)
XLA Ops:
  0.0 0.1 pad_add_fusion.place
  0.1 0.0 copy-start
  0.1 1.5 %copy-done = f32[2,896,256]{2,1,0:T(8,128)S(1)} copy-done((f32[2,896,256]{2,1,0:T(8,128)S(1)}, f32[2,896,256]{2,1,0:T(8,128)}, u32[]{:S(2)}) %copy-start) | copy-done | bytes 1835032
  1.6 0.0 copy-start.2
  1.6 1.3 %copy-done.2 = f32[896,384]{1,0:T(8,128)S(1)} copy-done((f32[896,384]{1,0:T(8,128)S(1)}, f32[896,384]{1,0:T(8,128)}, u32[]{:S(2)}) %copy-start.2) | copy-done | bytes 1376280
  2.9 0.0 copy-start.4
  2.9 0.7 copy-done.4
  3.6 7.0 %shard_map.37 = (f32[16,12,8,128]{3,2,1,0:T(8,128)S(1)}, f32[16,12,8,128]{3,2,1,0:T(8,128)S(1)}) custom-call(s32[2,256]{1,0:T(2,128)S(1)} %copy-done.4, s32[2]{0:T(128)S(1)} %pad_add_fusion.place, f32[896,384]{1,0:T(8,128)S(1)} %copy-done.2, f32[2,896,256]{2,1,0:T(8,128)S(1)} %copy-done), custom_call_target="tpu_custom_call" | custom-call | tf_op jit(solution)/shard_map/pallas_call | solution.py:72
  10.6 8.8 %collective-permute-start = (f32[16,12,8,128]{3,2,1,0:T(8,128)S(1)}, f32[16,12,8,128]{3,2,1,0:T(8,128)S(1)}, u32[]{:S(2)}, u32[]{:S(2)}) collective-permute-start(f32[16,12,8,128]{3,2,1,0:T(8,128)S(1)} %get-tuple-element.8), channel_id=1, source_target_pairs={{0,8},{8,0},{1,9},{9,1},{2,10},{10,2},{3,11},{11,3},{4,12},{12,4},... | collective-permute-start | bytes 2359304 | tf_op jit(solution)/shard_map/ppermute | solution.py:182
  19.4 1.9 %collective-permute-done = f32[16,12,8,128]{3,2,1,0:T(8,128)S(1)} collective-permute-done((f32[16,12,8,128]{3,2,1,0:T(8,128)S(1)}, f32[16,12,8,128]{3,2,1,0:T(8,128)S(1)}, u32[]{:S(2)}, u32[]{:S(2)}) %collective-permute-start) | collective-permute-done | bytes 786464 | tf_op jit(solution)/shard_map/ppermute | solution.py:182
  21.3 0.1 add.21
  21.3 17.4 %all_to_all.20 = f32[16,12,8,128]{3,2,1,0:T(8,128)} all-to-all(f32[16,12,8,128]{3,2,1,0:T(8,128)S(1)} %add.21), channel_id=1, replica_groups=mesh['z_hi'=2,'y'=4,'x'=4,'core'=2,'z_lo'=8] {'y','x'}, dimensions={0} | all-to-all | bytes 1572864 | tf_op jit(solution)/shard_map/all_to_all | solution.py:183
  38.7 0.0 copy-start.1
  38.7 0.0 copy-start.3
  38.7 1.3 %reduce_sum.18 = f32[12,8,128]{2,1,0:T(8,128)S(1)} reduce(f32[16,12,8,128]{3,2,1,0:T(8,128)} %all_to_all.20, f32[]{:T(128)} %constant.34.clone.1), dimensions={0}, to_apply=%region_0.0 | reduce | flops 184320 | bytes 835588 | tf_op jit(solution)/shard_map/reduce_sum | solution.py:183
  40.1 24.0 %all_to_all.21 = f32[16,8,128]{2,1,0:T(8,128)S(1)} all-to-all(f32[16,8,128]{2,1,0:T(8,128)S(1)} %concatenate.3), channel_id=1, replica_groups=mesh['z_hi'=2,'y'=4,'x'=4,'core'=2,'z_lo'=8] {'z_hi','z_lo'}, dimensions={0} | all-to-all | bytes 131072 | tf_op jit(solution)/shard_map/all_to_all | solution.py:186
  64.1 14.4 %all_to_all.22 = f32[16,8,128]{2,1,0:T(8,128)S(1)} all-to-all(f32[16,8,128]{2,1,0:T(8,128)S(1)} %broadcast_in_dim.7), channel_id=1, replica_groups=mesh['z_hi'=2,'y'=4,'x'=4,'core'=2,'z_lo'=8] {'z_hi','z_lo'}, dimensions={0} | all-to-all | bytes 131072 | tf_op jit(solution)/shard_map/all_to_all | solution.py:187
  78.5 0.1 broadcast_in_dim.8
  78.6 14.1 %all_to_all.23.mine = f32[16,12,8,128]{3,2,1,0:T(8,128)S(1)} all-to-all(f32[16,12,8,128]{3,2,1,0:T(8,128)S(1)} %broadcast_in_dim.8), channel_id=1, replica_groups=mesh['z_hi'=2,'y'=4,'x'=4,'core'=2,'z_lo'=8] {'y','x'}, dimensions={0} | all-to-all | bytes 1572864 | tf_op jit(solution)/shard_map/all_to_all | solution.py:188
  92.7 6.4 %collective-permute-start.1 = (f32[16,12,8,128]{3,2,1,0:T(8,128)S(1)}, f32[16,12,8,128]{3,2,1,0:T(8,128)S(1)}, u32[]{:S(2)}, u32[]{:S(2)}) collective-permute-start(f32[16,12,8,128]{3,2,1,0:T(8,128)S(1)} %all_to_all.23.mine), channel_id=1, source_target_pairs={{0,8},{8,0},{1,9},{9,1},{2,10},{10,2},{3,11},{11,3},{4,12},{12,4},... | collective-permute-start | bytes 2359304 | tf_op jit(solution)/shard_map/ppermute | solution.py:189
  99.0 1.9 %collective-permute-done.1.other = f32[16,12,8,128]{3,2,1,0:T(8,128)S(1)} collective-permute-done((f32[16,12,8,128]{3,2,1,0:T(8,128)S(1)}, f32[16,12,8,128]{3,2,1,0:T(8,128)S(1)}, u32[]{:S(2)}, u32[]{:S(2)}) %collective-permute-start.1) | collective-permute-done | bytes 786464 | tf_op jit(solution)/shard_map/ppermute | solution.py:189
  100.9 0.0 copy-done.1
  100.9 0.0 copy-done.3
  100.9 29.3 %shard_map.38 = f32[2,896,256]{2,1,0:T(8,128)} custom-call(s32[2]{0:T(128)S(1)} %pad_add_fusion.place, f32[16,12,8,128]{3,2,1,0:T(8,128)S(1)} %all_to_all.23.mine, f32[16,12,8,128]{3,2,1,0:T(8,128)S(1)} %collective-permute-done.1.other, f32[896,384]{1,0:T(8,128)S(1)} %copy-done.3, f32[2,896,256]{2,1,0:T(8,128)S(1)} %copy-done.1), custom_call_target="tpu_custom_call" | custom-call | tf_op jit(solution)/shard_map/pallas_call | solution.py:163
  (4 shorter events, 0.0 us)
Async XLA Ops:
  0.1 1.5 %copy-start = (f32[2,896,256]{2,1,0:T(8,128)S(1)}, f32[2,896,256]{2,1,0:T(8,128)}, u32[]{:S(2)}) copy-start(f32[2,896,256]{2,1,0:T(8,128)} %raw.3) | copy-start | bytes 5505028
  1.6 1.3 %copy-start.2 = (f32[896,384]{1,0:T(8,128)S(1)}, f32[896,384]{1,0:T(8,128)}, u32[]{:S(2)}) copy-start(f32[896,384]{1,0:T(8,128)} %prior.3) | copy-start | bytes 4128772
  2.9 0.7 copy-start.4
  10.6 10.7 %collective-permute-start = (f32[16,12,8,128]{3,2,1,0:T(8,128)S(1)}, f32[16,12,8,128]{3,2,1,0:T(8,128)S(1)}, u32[]{:S(2)}, u32[]{:S(2)}) collective-permute-start(f32[16,12,8,128]{3,2,1,0:T(8,128)S(1)} %get-tuple-element.8), channel_id=1, source_target_pairs={{0,8},{8,0},{1,9},{9,1},{2,10},{10,2},{3,11},{11,3},{4,12},{12,4},... | collective-permute-start | bytes 2359304 | tf_op jit(solution)/shard_map/ppermute | solution.py:182
  38.7 62.2 %copy-start.1 = (f32[2,896,256]{2,1,0:T(8,128)S(1)}, f32[2,896,256]{2,1,0:T(8,128)}, u32[]{:S(2)}) copy-start(f32[2,896,256]{2,1,0:T(8,128)} %raw.3) | copy-start | bytes 5505028
  38.7 62.2 %copy-start.3 = (f32[896,384]{1,0:T(8,128)S(1)}, f32[896,384]{1,0:T(8,128)}, u32[]{:S(2)}) copy-start(f32[896,384]{1,0:T(8,128)} %prior.3) | copy-start | bytes 4128772
  92.7 8.3 %collective-permute-start.1 = (f32[16,12,8,128]{3,2,1,0:T(8,128)S(1)}, f32[16,12,8,128]{3,2,1,0:T(8,128)S(1)}, u32[]{:S(2)}, u32[]{:S(2)}) collective-permute-start(f32[16,12,8,128]{3,2,1,0:T(8,128)S(1)} %all_to_all.23.mine), channel_id=1, source_target_pairs={{0,8},{8,0},{1,9},{9,1},{2,10},{10,2},{3,11},{11,3},{4,12},{12,4},... | collective-permute-start | bytes 2359304 | tf_op jit(solution)/shard_map/ppermute | solution.py:189

commit v2 on v1

--- a/solution.py
+++ b/solution.py
@@ -13,6 +13,7 @@
 AXES = ("z_hi", "y", "x", "core", "z_lo")
 TILE = (8, 128)
 VMEM_LIMIT = 48 * 1024 * 1024
+PACK_VMEM_LIMIT = 60 * 1024 * 1024
 
 
 def dot(left, right, left_dim=1, right_dim=0):
@@ -20,65 +21,81 @@
     return lax.dot_general(left, right, dims, precision=HIGHEST, preferred_element_type=F32)
 
 
-def pack_kernel(pivots, place, prior, raw, keep, send):
+def pack_kernel(pivots, place, prior, raw, keep, send, counts, sem):
     keep[...] = jnp.zeros_like(keep)
     send[...] = jnp.zeros_like(send)
     offset, core = place[0], place[1]
-    rows_here = prior.shape[0]
-    groups = keep.shape[0]
-    half = groups * 8
+    rows_here = jnp.uint32(prior.shape[0])
+    per_step = pivots.shape[1]
+    chunk = 8
+
+    def local(step, pivot):
+        row = pivots[step, pivot] - offset
+        return row, row.astype(jnp.uint32) < rows_here
+
+    def tiles(step):
+        base = 5 * step
+        for t in range(3):
+            yield base + t, prior, 128 * t
+        for which in range(step + 1):
+            for t in range(2):
+                yield base + 3 + 2 * which + t, raw.at[which], 128 * t
+
+    def copy(source, row, column, target):
+        return pltpu.make_async_copy(source.at[pl.ds(row, 1), pl.ds(column, 128)], target, sem)
+
+    def start(step, pivot):
+        row, here = local(step, pivot)
+
+        @pl.when(here)
+        def _():
+            counts[step] += 1
+            half = keep.shape[0]
+            group, line = pivot // 8, pl.ds(lax.rem(pivot, 8), 1)
+            for side, target in ((core, keep), (1 - core, send)):
+
+                @pl.when(group // half == side)
+                def _():
+                    for number, source, column in tiles(step):
+                        copy(source, row, column, target.at[lax.rem(group, half), number, line]).start()
 
     for step in range(2):
-        base = 5 * step
-
-        def look(pivot, step=step, base=base):
-            row = pivots[step, pivot] - offset
-            here = jnp.logical_and(row >= 0, row < rows_here)
-
-            @pl.when(here)
-            def _():
-                side = pivot // half
-                group = lax.rem(pivot, half) // 8
-                line = pl.ds(lax.rem(pivot, 8), 1)
-
-                def put(target):
-                    values = prior[pl.ds(row, 1), :]
-                    for t in range(3):
-                        target[group, base + t, line, :] = values[:, 128 * t : 128 * t + 128]
-                    for which in range(step + 1):
-                        values = raw[which, pl.ds(row, 1), :]
-                        for t in range(2):
-                            target[group, base + 3 + 2 * which + t, line, :] = values[:, 128 * t : 128 * t + 128]
-
-                @pl.when(side == core)
-                def _():
-                    put(keep)
-
-                @pl.when(side != core)
-                def _():
-                    put(send)
-
-        def chunk(which, _):
-            for k in range(8):
-                look(which * 8 + k)
-            return 0
-
-        lax.fori_loop(0, pivots.shape[1] // 8, chunk, 0)
+        counts[step] = 0
+
+        for first in range(0, per_step, chunk):
+            found = local(step, first)[1]
+            for k in range(1, chunk):
+                found = jnp.logical_or(found, local(step, first + k)[1])
+
+            @pl.when(found)
+            def _(step=step, first=first):
+                lax.fori_loop(0, chunk, lambda k, _: start(step, first + k), None)
+
+    for step in range(2):
+
+        def finish(_, carry, step=step):
+            for _, source, column in tiles(step):
+                copy(source, 0, column, keep.at[0, 0, pl.ds(0, 1)]).wait()
+            return carry
+
+        lax.fori_loop(0, counts[step], finish, 0)
 
 
 def pack(pivot_rows, place, prior, raw, groups):
     shape = jax.ShapeDtypeStruct((groups, 12) + TILE, F32)
     vmem, smem = pl.BlockSpec(memory_space=pltpu.VMEM), pl.BlockSpec(memory_space=pltpu.SMEM)
+    where_it_is = pl.BlockSpec(memory_space=pl.ANY)
     return pl.pallas_call(
         pack_kernel,
         out_shape=(shape, shape),
-        in_specs=[smem, smem, vmem, vmem],
+        in_specs=[smem, smem, where_it_is, where_it_is],
         out_specs=(vmem, vmem),
-        compiler_params=pltpu.CompilerParams(vmem_limit_bytes=VMEM_LIMIT),
+        scratch_shapes=[pltpu.SMEM((2,), jnp.int32), pltpu.SemaphoreType.DMA],
+        compiler_params=pltpu.CompilerParams(vmem_limit_bytes=PACK_VMEM_LIMIT),
     )(pivot_rows, place, prior, raw)
 
 
-def eliminate(block, panel):
+def eliminate(block, panel, beside):
     width = block.shape[0]
     lanes = 2 * width
     row_of = lax.broadcasted_iota(jnp.int32, (width, width), 0)
@@ -91,8 +108,7 @@
         rows, scaled = [], []
         for k in range(panel):
             pivot = jnp.broadcast_to(columns[k][k : k + 1], TILE)
-            root = lax.rsqrt(pivot)
-            root = (root * (1.5 - 0.5 * pivot * root * root))[0:1]
+            root = lax.rsqrt(pivot)[0:1]
             row = work[k : k + 1]
             for before in range(k):
                 row = row - scaled[before][k : k + 1] * rows[before]
@@ -101,6 +117,7 @@
             for after in range(k + 1, panel):
                 columns[after] = columns[after] - scaled[k] * (columns[after][k : k + 1] * root)
         done.extend(rows)
+        beside()
         if left > panel:
             work = work[panel:]
             for k in range(panel):
@@ -108,7 +125,7 @@
     return jnp.concatenate(done, axis=0)[:, width:]
 
 
-def cholesky_inverse(symmetric, width=64, panel=16):
+def cholesky_inverse(symmetric, beside, width=64, panel=16):
     size = symmetric.shape[0]
     work = symmetric
     finished = []
@@ -116,7 +133,7 @@
         low = which * width
         rest = size - low - width
         line = work[:width]
-        inverse = eliminate(line[:, low : low + width], panel)
+        inverse = eliminate(line[:, low : low + width], panel, beside)
         parts = [inverse]
         if low:
             parts.insert(0, jnp.zeros((width, low), F32))
@@ -142,19 +159,42 @@
         return jnp.concatenate(tiles, axis=1)
 
     prior_0, prior_1 = columns(0, 3), columns(5, 3)
-    vectors = prior[...]
+    rows_here = prior.shape[0]
+    chunks = [slice(rows_here * c // 4, rows_here * (c + 1) // 4) for c in range(4)]
 
     def symmetrized(block):
         return 0.5 * (block + block.T)
 
-    inverse_0 = cholesky_inverse(symmetrized(columns(3, 2) - dot(prior_0, prior_0, 1, 1)))
+    def residual(step, pivots, rows):
+        out[step, rows] = raw[step, rows] - dot(prior[rows], pivots, 1, 1)
+
+    def finish(step, inverse, rows):
+        out[step, rows] = dot(out[step, rows], inverse, 1, 1)
+
+    def take(pivots, rows):
+        out[1, rows] = out[1, rows] - dot(out[0, rows], pivots, 1, 1)
+
+    def beside(tasks):
+        calls = iter(range(1000))
+
+        def call():
+            if next(calls) % 2 == 0 and tasks:
+                tasks.pop(0)()
+
+        return call
+
+    tasks = [functools.partial(residual, 0, prior_0, rows) for rows in chunks]
+    tasks += [functools.partial(residual, 1, prior_1, rows) for rows in chunks]
+    inverse_0 = cholesky_inverse(symmetrized(columns(3, 2) - dot(prior_0, prior_0, 1, 1)), beside(tasks))
     fresh_pivots = dot(columns(8, 2) - dot(prior_1, prior_0, 1, 1), inverse_0, 1, 1)
     block_1 = columns(10, 2) - dot(prior_1, prior_1, 1, 1) - dot(fresh_pivots, fresh_pivots, 1, 1)
-    inverse_1 = cholesky_inverse(symmetrized(block_1))
-    fresh = dot(raw[0] - dot(vectors, prior_0, 1, 1), inverse_0, 1, 1)
-    out[0] = fresh
-    residual = raw[1] - dot(vectors, prior_1, 1, 1) - dot(fresh, fresh_pivots, 1, 1)
-    out[1] = dot(residual, inverse_1, 1, 1)
+    tasks += [functools.partial(finish, 0, inverse_0, rows) for rows in chunks]
+    tasks += [functools.partial(take, fresh_pivots, rows) for rows in chunks]
+    inverse_1 = cholesky_inverse(symmetrized(block_1), beside(tasks))
+    for task in tasks:
+        task()
+    for rows in chunks:
+        finish(1, inverse_1, rows)
 
 
 def steps(place, mine, other, prior, raw):

time: 131 us -> 119 us (0.908)
  Pallas kernels: 36.3 us -> 26 us
  local copies, waits for them, and re-layouts: 3.61 us -> 0.1 us
  other arithmetic: 1.52 us -> 3.13 us
    pallas_call x1, Pallas kernels: 29.3 us -> 23.1 us  [steps(): pl.pallas_call(steps_kernel, out_shape=jax.ShapeDtypeStruct(raw.shape, F3...]
    pallas_call x1, Pallas kernels: 6.98 us -> 2.9 us  [pack(): pl.pallas_call(pack_kernel, out_shape=(shape, shape), in_specs=[smem, sme...]
    unnamed x10 -> x6, local copies, waits for them, and re-layouts: 3.53 us -> 0.01 us
where the time goes in v2:
time: 119 us
  blocking collectives  70.4 us (59%)
  Pallas kernels  26 us (22%)
  starting transfers between devices  15.5 us (13%)
  waiting for transfers between devices  3.81 us (3%)
  other arithmetic  3.13 us (3%)
    all_to_all x1, blocking collectives, body(): total = jnp.sum(lax.all_to_all(total, line, 0, 0), axis=0)  24.9 us
    pallas_call x1, Pallas kernels, steps(): pl.pallas_call(steps_kernel, out_shape=jax.ShapeDtypeStruct(raw.shape, F3...  23.1 us
    all_to_all x1, blocking collectives, body(): total = jnp.sum(lax.all_to_all(total, plane, 0, 0), axis=0)  17.4 us
    all_to_all x1, blocking collectives, body(): lax.all_to_all(jnp.broadcast_to(total, (in_line,) + TILE), line, 0, 0)  14.3 us
    all_to_all x1, blocking collectives, body(): lax.all_to_all(jnp.broadcast_to(total, (in_plane,) + total.shape), plane,...  13.9 us
    ppermute x1, starting transfers between devices, body(): total = keep + lax.ppermute(send, 'core', swap)  8.93 us
    ppermute x1, starting transfers between devices, body(): other = lax.ppermute(mine, 'core', swap)  6.53 us
    pallas_call x1, Pallas kernels, pack(): pl.pallas_call(pack_kernel, out_shape=(shape, shape), in_specs=[smem, sme...  2.9 us
  transfers between devices with their start and end apart: 2, of which 2 were waited for; matrix products, arithmetic and copies ran while one was open for 0% of the time, Pallas kernels for 0%

profile of v2, /device:TPU:1, one launch (start us, length us, event | category | flops | bytes accessed | tf_op | source)
XLA Modules:
  0.0 119.0 jit_solution(9936689107571199464)
XLA Ops:
  0.0 0.6 pad_add_fusion.place
  0.6 2.9 %shard_map.37 = (f32[16,12,8,128]{3,2,1,0:T(8,128)}, f32[16,12,8,128]{3,2,1,0:T(8,128)}) custom-call(s32[2,256]{1,0:T(2,128)} %pivots.1, s32[2]{0:T(128)} %pad_add_fusion.place, f32[896,384]{1,0:T(8,128)} %prior.3, f32[2,896,256]{2,1,0:T(8,128)} %raw.3), custom_call_target="tpu_custom_call" | custom-call | tf_op jit(solution)/shard_map/pallas_call | solution.py:88
  3.5 8.9 %collective-permute-start = (f32[16,12,8,128]{3,2,1,0:T(8,128)}, f32[16,12,8,128]{3,2,1,0:T(8,128)S(1)}, u32[]{:S(2)}, u32[]{:S(2)}) collective-permute-start(f32[16,12,8,128]{3,2,1,0:T(8,128)} %get-tuple-element.8), channel_id=1, source_target_pairs={{0,8},{8,0},{1,9},{9,1},{2,10},{10,2},{3,11},{11,3},{4,12},{12,4},... | collective-permute-start | bytes 2359304 | tf_op jit(solution)/shard_map/ppermute | solution.py:222
  12.4 2.1 %collective-permute-done = f32[16,12,8,128]{3,2,1,0:T(8,128)S(1)} collective-permute-done((f32[16,12,8,128]{3,2,1,0:T(8,128)}, f32[16,12,8,128]{3,2,1,0:T(8,128)S(1)}, u32[]{:S(2)}, u32[]{:S(2)}) %collective-permute-start) | collective-permute-done | bytes 786464 | tf_op jit(solution)/shard_map/ppermute | solution.py:222
  14.5 1.2 %add.21 = f32[16,12,8,128]{3,2,1,0:T(8,128)S(1)} add(f32[16,12,8,128]{3,2,1,0:T(8,128)} %get-tuple-element.7, f32[16,12,8,128]{3,2,1,0:T(8,128)S(1)} %collective-permute-done) | non-fusion elementwise | flops 196608 | bytes 2359296 | tf_op jit(solution)/shard_map/add | solution.py:222
  15.7 17.4 %all_to_all.20 = f32[16,12,8,128]{3,2,1,0:T(8,128)} all-to-all(f32[16,12,8,128]{3,2,1,0:T(8,128)S(1)} %add.21), channel_id=1, replica_groups=mesh['z_hi'=2,'y'=4,'x'=4,'core'=2,'z_lo'=8] {'y','x'}, dimensions={0} | all-to-all | bytes 1572864 | tf_op jit(solution)/shard_map/all_to_all | solution.py:223
  33.1 0.0 copy-start
  33.1 0.0 copy-start.1
  33.1 0.0 copy-start.2
  33.1 1.3 %reduce_sum.18 = f32[12,8,128]{2,1,0:T(8,128)S(1)} reduce(f32[16,12,8,128]{3,2,1,0:T(8,128)} %all_to_all.20, f32[]{:T(128)} %constant.34.clone.1), dimensions={0}, to_apply=%region_0.0 | reduce | flops 184320 | bytes 835588 | tf_op jit(solution)/shard_map/reduce_sum | solution.py:223
  34.5 24.9 %all_to_all.21 = f32[16,8,128]{2,1,0:T(8,128)S(1)} all-to-all(f32[16,8,128]{2,1,0:T(8,128)S(1)} %concatenate.3), channel_id=1, replica_groups=mesh['z_hi'=2,'y'=4,'x'=4,'core'=2,'z_lo'=8] {'z_hi','z_lo'}, dimensions={0} | all-to-all | bytes 131072 | tf_op jit(solution)/shard_map/all_to_all | solution.py:226
  59.4 14.3 %all_to_all.22 = f32[16,8,128]{2,1,0:T(8,128)S(1)} all-to-all(f32[16,8,128]{2,1,0:T(8,128)S(1)} %broadcast_in_dim.7), channel_id=1, replica_groups=mesh['z_hi'=2,'y'=4,'x'=4,'core'=2,'z_lo'=8] {'z_hi','z_lo'}, dimensions={0} | all-to-all | bytes 131072 | tf_op jit(solution)/shard_map/all_to_all | solution.py:227
  73.7 0.1 broadcast_in_dim.8
  73.7 13.9 %all_to_all.23.mine = f32[16,12,8,128]{3,2,1,0:T(8,128)S(1)} all-to-all(f32[16,12,8,128]{3,2,1,0:T(8,128)S(1)} %broadcast_in_dim.8), channel_id=1, replica_groups=mesh['z_hi'=2,'y'=4,'x'=4,'core'=2,'z_lo'=8] {'y','x'}, dimensions={0} | all-to-all | bytes 1572864 | tf_op jit(solution)/shard_map/all_to_all | solution.py:228
  87.6 6.5 %collective-permute-start.1 = (f32[16,12,8,128]{3,2,1,0:T(8,128)S(1)}, f32[16,12,8,128]{3,2,1,0:T(8,128)S(1)}, u32[]{:S(2)}, u32[]{:S(2)}) collective-permute-start(f32[16,12,8,128]{3,2,1,0:T(8,128)S(1)} %all_to_all.23.mine), channel_id=1, source_target_pairs={{0,8},{8,0},{1,9},{9,1},{2,10},{10,2},{3,11},{11,3},{4,12},{12,4},... | collective-permute-start | bytes 2359304 | tf_op jit(solution)/shard_map/ppermute | solution.py:229
  94.2 1.7 %collective-permute-done.1.other = f32[16,12,8,128]{3,2,1,0:T(8,128)S(1)} collective-permute-done((f32[16,12,8,128]{3,2,1,0:T(8,128)S(1)}, f32[16,12,8,128]{3,2,1,0:T(8,128)S(1)}, u32[]{:S(2)}, u32[]{:S(2)}) %collective-permute-start.1) | collective-permute-done | bytes 786464 | tf_op jit(solution)/shard_map/ppermute | solution.py:229
  95.9 0.0 copy-done
  95.9 0.0 copy-done.1
  95.9 0.0 copy-done.2
  95.9 23.1 %shard_map.38 = f32[2,896,256]{2,1,0:T(8,128)} custom-call(s32[2]{0:T(128)S(1)} %copy-done.2, f32[16,12,8,128]{3,2,1,0:T(8,128)S(1)} %all_to_all.23.mine, f32[16,12,8,128]{3,2,1,0:T(8,128)S(1)} %collective-permute-done.1.other, f32[896,384]{1,0:T(8,128)S(1)} %copy-done.1, f32[2,896,256]{2,1,0:T(8,128)S(1)} %copy-done), custom_call_target="tpu_custom_call" | custom-call | tf_op jit(solution)/shard_map/pallas_call | solution.py:203
  (4 shorter events, 0.0 us)
Async XLA Ops:
  3.5 11.0 %collective-permute-start = (f32[16,12,8,128]{3,2,1,0:T(8,128)}, f32[16,12,8,128]{3,2,1,0:T(8,128)S(1)}, u32[]{:S(2)}, u32[]{:S(2)}) collective-permute-start(f32[16,12,8,128]{3,2,1,0:T(8,128)} %get-tuple-element.8), channel_id=1, source_target_pairs={{0,8},{8,0},{1,9},{9,1},{2,10},{10,2},{3,11},{11,3},{4,12},{12,4},... | collective-permute-start | bytes 2359304 | tf_op jit(solution)/shard_map/ppermute | solution.py:222
  33.1 62.8 %copy-start = (f32[2,896,256]{2,1,0:T(8,128)S(1)}, f32[2,896,256]{2,1,0:T(8,128)}, u32[]{:S(2)}) copy-start(f32[2,896,256]{2,1,0:T(8,128)} %raw.3) | copy-start | bytes 5505028
  33.1 62.8 %copy-start.1 = (f32[896,384]{1,0:T(8,128)S(1)}, f32[896,384]{1,0:T(8,128)}, u32[]{:S(2)}) copy-start(f32[896,384]{1,0:T(8,128)} %prior.3) | copy-start | bytes 4128772
  33.1 62.8 %copy-start.2 = (s32[2]{0:T(128)S(1)}, s32[2]{0:T(128)}, u32[]{:S(2)}) copy-start(s32[2]{0:T(128)} %pad_add_fusion.place) | copy-start | bytes 28
  87.6 8.2 %collective-permute-start.1 = (f32[16,12,8,128]{3,2,1,0:T(8,128)S(1)}, f32[16,12,8,128]{3,2,1,0:T(8,128)S(1)}, u32[]{:S(2)}, u32[]{:S(2)}) collective-permute-start(f32[16,12,8,128]{3,2,1,0:T(8,128)S(1)} %all_to_all.23.mine), channel_id=1, source_target_pairs={{0,8},{8,0},{1,9},{9,1},{2,10},{10,2},{3,11},{11,3},{4,12},{12,4},... | collective-permute-start | bytes 2359304 | tf_op jit(solution)/shard_map/ppermute | solution.py:229

commit v3 on v2

v3 whole, which is shorter than its diff:
```python
import functools

import jax
import jax.numpy as jnp
from jax import lax
from jax.experimental import pallas as pl
from jax.experimental.pallas import tpu as pltpu
from jax.sharding import Mesh
from jax.sharding import PartitionSpec as P

F32 = jnp.float32
HIGHEST = lax.Precision.HIGHEST
AXES = ("z_hi", "y", "x", "core", "z_lo")
TILE = (8, 128)
VMEM_LIMIT = 48 * 1024 * 1024
PACK_VMEM_LIMIT = 60 * 1024 * 1024


def dot(left, right, left_dim=1, right_dim=0):
    dims = (((left_dim,), (right_dim,)), ((), ()))
    return lax.dot_general(left, right, dims, precision=HIGHEST, preferred_element_type=F32)


def pack_kernel(pivots, prior, raw, keep, send, counts, sem):
    keep[...] = jnp.zeros_like(keep)
    send[...] = jnp.zeros_like(send)
    rows_here = prior.shape[0]
    offset, core = lax.axis_index(AXES) * rows_here, lax.axis_index("core")
    per_step = pivots.shape[1]
    chunk = 8

    def local(step, pivot):
        row = pivots[step, pivot] - offset
        return row, row.astype(jnp.uint32) < jnp.uint32(rows_here)

    def tiles(step):
        base = 5 * step
        for t in range(3):
            yield base + t, prior, 128 * t
        for which in range(step + 1):
            for t in range(2):
                yield base + 3 + 2 * which + t, raw.at[which], 128 * t

    def copy(source, row, column, target):
        return pltpu.make_async_copy(source.at[pl.ds(row, 1), pl.ds(column, 128)], target, sem)

    def start(step, pivot):
        row, here = local(step, pivot)

        @pl.when(here)
        def _():
            counts[step] += 1
            half = keep.shape[0]
            group, line = pivot // 8, pl.ds(lax.rem(pivot, 8), 1)
            for side, target in ((core, keep), (1 - core, send)):

                @pl.when(group // half == side)
                def _():
                    for number, source, column in tiles(step):
                        copy(source, row, column, target.at[lax.rem(group, half), number, line]).start()

    for step in range(2):
        counts[step] = 0

        for first in range(0, per_step, chunk):
            found = local(step, first)[1]
            for k in range(1, chunk):
                found = jnp.logical_or(found, local(step, first + k)[1])

            @pl.when(found)
            def _(step=step, first=first):
                lax.fori_loop(0, chunk, lambda k, _: start(step, first + k), None)

    for step in range(2):

        def finish(_, carry, step=step):
            for _, source, column in tiles(step):
                copy(source, 0, column, keep.at[0, 0, pl.ds(0, 1)]).wait()
            return carry

        lax.fori_loop(0, counts[step], finish, 0)


def pack(pivot_rows, prior, raw, groups):
    shape = jax.ShapeDtypeStruct((groups, 12) + TILE, F32)
    vmem, smem = pl.BlockSpec(memory_space=pltpu.VMEM), pl.BlockSpec(memory_space=pltpu.SMEM)
    where_it_is = pl.BlockSpec(memory_space=pl.ANY)
    return pl.pallas_call(
        pack_kernel,
        out_shape=(shape, shape),
        in_specs=[smem, where_it_is, where_it_is],
        out_specs=(vmem, vmem),
        scratch_shapes=[pltpu.SMEM((2,), jnp.int32), pltpu.SemaphoreType.DMA],
        compiler_params=pltpu.CompilerParams(vmem_limit_bytes=PACK_VMEM_LIMIT),
    )(pivot_rows, prior, raw)


def spread(line):
    return jnp.broadcast_to(line, TILE)


def eliminate(block, at, beside):
    width = block.shape[0]
    row_of = lax.broadcasted_iota(jnp.int32, (width, width), 0)
    column_of = lax.broadcasted_iota(jnp.int32, (width, width), 1)
    line_of = lax.broadcasted_iota(jnp.int32, TILE, 0)
    halves = [block, (row_of == column_of).astype(F32)]
    work = jnp.concatenate(halves[:: -1 if at else 1], axis=1)
    done = []
    columns = [jnp.broadcast_to(work[:8, at + k : at + k + 1], TILE) for k in range(8)]
    for first in range(0, width, 8):
        left = width - first
        below = left // 8 - 1
        head, finished, rows, under, after = work[:8], work[:8], [], [], []
        if below:
            for k in range(8, 16):
                after.append(jnp.broadcast_to(work[8:16, at + first + k : at + first + k + 1], TILE))
            for k in range(8):
                column = jnp.broadcast_to(work[8:, at + first + k : at + first + k + 1], (left - 8, 128))
                under.append(column.reshape((below,) + TILE))
        for k in range(8):
            root = lax.rsqrt(spread(columns[k][k : k + 1]))
            scaled = columns[k] * root
            rows.append(spread(head[k : k + 1]) * root)
            finished = jnp.where(line_of == k, rows[k], finished)
            if k < 7:
                head = head - scaled * rows[k]
            if below:
                under[k] = under[k] * root
            for m in range(k + 1, 8):
                factor = spread(scaled[m : m + 1])
                columns[m] = columns[m] - scaled * factor
                if below:
                    under[m] = under[m] - under[k] * factor
        done.append(finished)
        if below:
            for k in range(8):
                column = under[k][0]
                for m in range(8):
                    after[m] = after[m] - column * spread(column[m : m + 1])
            columns = after
            work = work[8:].reshape((below,) + TILE)
            for k in range(8):
                work = work - under[k] * rows[k]
            work = work.reshape(left - 8, 128)
        beside()
    return jnp.concatenate(done, axis=0)


def cholesky_inverse(symmetric, beside):
    size, width = symmetric.shape[0], 64
    work = symmetric
    finished = []
    for which in range(size // width):
        low, high = which * width, (which + 1) * width
        at = low % 128
        rest = size - high
        block_of = lax.broadcasted_iota(jnp.int32, (width, size), 1) // width
        on_diagonal = lax.broadcasted_iota(jnp.int32, (width, size), 1) == lax.broadcasted_iota(jnp.int32, (width, size), 0) + low
        line = jnp.where(block_of == which, on_diagonal.astype(F32), work[:width])
        blank = jnp.zeros_like(line)
        line = jnp.concatenate([blank, line] if at == 0 else [line, blank], axis=0)
        inverse = eliminate(work[:width, low:high], at, beside)
        if rest:
            column = work[width:, low:high]
            blank = jnp.zeros_like(column)
            column = jnp.concatenate([blank, column] if at == 0 else [column, blank], axis=1)
            factor = dot(column, inverse, 1, 1)
            block_of_rest = lax.broadcasted_iota(jnp.int32, (rest, size), 1) // width
            work = jnp.where(block_of_rest == which, 0.0, work[width:])
        line = dot(inverse, line)
        if rest:
            work = work - dot(factor, line)
        finished.append(jnp.where(block_of <= which, line, 0.0))
    return jnp.concatenate(finished, axis=0)


def steps_kernel(mine, other, prior, raw, out, packed):
    core = lax.axis_index("core")
    half = mine.shape[0]
    packed[pl.ds(core * half, half)] = mine[...]
    packed[pl.ds((1 - core) * half, half)] = other[...]

    def columns(first, count):
        tiles = [packed[:, first + t].reshape(2 * half * 8, 128) for t in range(count)]
        return jnp.concatenate(tiles, axis=1)

    prior_0, prior_1 = columns(0, 3), columns(5, 3)
    rows_here = prior.shape[0]
    chunks = [slice(rows_here * c // 4, rows_here * (c + 1) // 4) for c in range(4)]

    def symmetrized(block):
        return 0.5 * (block + block.T)

    def residual(step, pivots, rows):
        out[step, rows] = raw[step, rows] - dot(prior[rows], pivots, 1, 1)

    def finish(step, inverse, rows):
        out[step, rows] = dot(out[step, rows], inverse, 1, 1)

    def take(pivots, rows):
        out[1, rows] = out[1, rows] - dot(out[0, rows], pivots, 1, 1)

    def beside(tasks):
        calls = iter(range(1000))

        def call():
            if next(calls) % 3 == 0 and tasks:
                tasks.pop(0)()

        return call

    tasks = [functools.partial(residual, 0, prior_0, rows) for rows in chunks]
    tasks += [functools.partial(residual, 1, prior_1, rows) for rows in chunks]
    later = {}

    def cross():
        later["cross"] = columns(8, 2) - dot(prior_1, prior_0, 1, 1)

    def block():
        later["block"] = symmetrized(columns(10, 2) - dot(prior_1, prior_1, 1, 1))

    tasks.insert(0, cross)
    tasks.insert(0, block)
    inverse_0 = cholesky_inverse(symmetrized(columns(3, 2) - dot(prior_0, prior_0, 1, 1)), beside(tasks))
    fresh_pivots = dot(later["cross"], inverse_0, 1, 1)
    block_1 = later["block"] - symmetrized(dot(fresh_pivots, fresh_pivots, 1, 1))
    tasks += [functools.partial(finish, 0, inverse_0, rows) for rows in chunks]
    tasks += [functools.partial(take, fresh_pivots, rows) for rows in chunks]
    inverse_1 = cholesky_inverse(block_1, beside(tasks))
    for task in tasks:
        task()
    for rows in chunks:
        finish(1, inverse_1, rows)


def steps(mine, other, prior, raw):
    vmem = pl.BlockSpec(memory_space=pltpu.VMEM)
    groups = mine.shape[0]
    return pl.pallas_call(
        steps_kernel,
        out_shape=jax.ShapeDtypeStruct(raw.shape, F32),
        in_specs=[vmem] * 4,
        out_specs=vmem,
        scratch_shapes=[pltpu.VMEM((2 * groups, 12) + TILE, F32)],
        compiler_params=pltpu.CompilerParams(vmem_limit_bytes=VMEM_LIMIT),
    )(mine, other, prior, raw)


def body(prior, raw, pivot_rows):
    plane, line = ("y", "x"), ("z_hi", "z_lo")
    in_plane = lax.axis_size(plane)
    swap = [(0, 1), (1, 0)]

    keep, send = pack(pivot_rows, prior, raw, in_plane)
    total = keep + lax.ppermute(send, "core", swap)
    total = jnp.sum(lax.all_to_all(total, plane, 0, 0), axis=0)
    for groups in ([[4 * run + k for k in range(4)] for run in range(4)], [[4 * run + k for run in range(4)] for k in range(4)]):
        copies = jnp.broadcast_to(total, (4,) + total.shape)
        total = jnp.sum(lax.all_to_all(copies, line, 0, 0, axis_index_groups=groups), axis=0)
    mine = lax.all_to_all(jnp.broadcast_to(total, (in_plane,) + total.shape), plane, 0, 0)
    other = lax.ppermute(mine, "core", swap)
    return steps(mine, other, prior, raw)


def solution(mesh):
    fine = Mesh(mesh.devices.reshape(2, 4, 4, 2, 8), AXES)
    return jax.shard_map(
        body,
        mesh=fine,
        in_specs=(P(AXES, None), P(None, AXES, None), P()),
        out_specs=P(None, AXES, None),
        check_vma=False,
    )
```

time: 119 us -> 110 us (0.924)
  Pallas kernels: 26 us -> 21.5 us
  blocking collectives: 70.4 us -> 67.1 us
  other arithmetic: 3.13 us -> 1.29 us
    pallas_call x1, Pallas kernels: 23.1 us -> 17.6 us  [steps(): pl.pallas_call(steps_kernel, out_shape=jax.ShapeDtypeStruct(raw.shape, F3...]
    all_to_all x2, blocking collectives: 39.2 us -> 36.4 us  [body(): lax.all_to_all(copies, line, 0, 0, axis_index_groups=groups)]
    reduce_sum x1, other arithmetic: 1.33 us -> 0.05 us  [body(): total = jnp.sum(lax.all_to_all(total, plane, 0, 0), axis=0)]
where the time goes in v3:
time: 110 us
  blocking collectives  67.1 us (61%)
  Pallas kernels  21.5 us (20%)
  starting transfers between devices  15.8 us (14%)
  waiting for transfers between devices  3.81 us (3%)
  other arithmetic  1.29 us (1%)
    all_to_all x2, blocking collectives, body(): lax.all_to_all(copies, line, 0, 0, axis_index_groups=groups)  36.4 us
    pallas_call x1, Pallas kernels, steps(): pl.pallas_call(steps_kernel, out_shape=jax.ShapeDtypeStruct(raw.shape, F3...  17.6 us
    all_to_all x1, blocking collectives, body(): total = jnp.sum(lax.all_to_all(total, plane, 0, 0), axis=0)  16.7 us
    all_to_all x1, blocking collectives, body(): lax.all_to_all(jnp.broadcast_to(total, (in_plane,) + total.shape), plane,...  14 us
    ppermute x1, starting transfers between devices, body(): total = keep + lax.ppermute(send, 'core', swap)  8.99 us
    ppermute x1, starting transfers between devices, body(): other = lax.ppermute(mine, 'core', swap)  6.84 us
    pallas_call x1, Pallas kernels, pack(): pl.pallas_call(pack_kernel, out_shape=(shape, shape), in_specs=[smem, whe...  3.89 us
  transfers between devices with their start and end apart: 2, of which 2 were waited for; matrix products, arithmetic and copies ran while one was open for 0% of the time, Pallas kernels for 0%

profile of v3, /device:TPU:1, one launch (start us, length us, event | category | flops | bytes accessed | tf_op | source)
XLA Modules:
  0.0 109.6 jit_solution(14391700955392755775)
XLA Ops:
  0.0 3.9 %shard_map.37 = (f32[16,12,8,128]{3,2,1,0:T(8,128)}, f32[16,12,8,128]{3,2,1,0:T(8,128)}) custom-call(s32[2,256]{1,0:T(2,128)} %pivots.1, f32[896,384]{1,0:T(8,128)} %prior.3, f32[2,896,256]{2,1,0:T(8,128)} %raw.3), custom_call_target="tpu_custom_call" | custom-call | tf_op jit(solution)/shard_map/pallas_call | solution.py:88
  3.9 9.0 %collective-permute-start = (f32[16,12,8,128]{3,2,1,0:T(8,128)}, f32[16,12,8,128]{3,2,1,0:T(8,128)S(1)}, u32[]{:S(2)}, u32[]{:S(2)}) collective-permute-start(f32[16,12,8,128]{3,2,1,0:T(8,128)} %get-tuple-element.8), channel_id=1, source_target_pairs={{0,8},{8,0},{1,9},{9,1},{2,10},{10,2},{3,11},{11,3},{4,12},{12,4},... | collective-permute-start | bytes 2359304 | tf_op jit(solution)/shard_map/ppermute | solution.py:256
  12.9 2.1 %collective-permute-done = f32[16,12,8,128]{3,2,1,0:T(8,128)S(1)} collective-permute-done((f32[16,12,8,128]{3,2,1,0:T(8,128)}, f32[16,12,8,128]{3,2,1,0:T(8,128)S(1)}, u32[]{:S(2)}, u32[]{:S(2)}) %collective-permute-start) | collective-permute-done | bytes 786464 | tf_op jit(solution)/shard_map/ppermute | solution.py:256
  15.0 1.2 %add.3 = f32[16,12,8,128]{3,2,1,0:T(8,128)S(1)} add(f32[16,12,8,128]{3,2,1,0:T(8,128)} %get-tuple-element.7, f32[16,12,8,128]{3,2,1,0:T(8,128)S(1)} %collective-permute-done) | non-fusion elementwise | flops 196608 | bytes 2359296 | tf_op jit(solution)/shard_map/add | solution.py:256
  16.2 16.7 %all_to_all.20 = f32[16,12,8,128]{3,2,1,0:T(8,128)S(1)} all-to-all(f32[16,12,8,128]{3,2,1,0:T(8,128)S(1)} %add.3), channel_id=1, replica_groups=mesh['z_hi'=2,'y'=4,'x'=4,'core'=2,'z_lo'=8] {'y','x'}, dimensions={0} | all-to-all | bytes 1572864 | tf_op jit(solution)/shard_map/all_to_all | solution.py:257
  33.0 8.7 %all_to_all.21 = f32[4,12,8,128]{3,2,1,0:T(8,128)S(1)} all-to-all(f32[4,12,8,128]{3,2,1,0:T(8,128)S(1)} %broadcast_in_dim.9), channel_id=1, replica_groups={{0,1,2,3},{4,5,6,7},{256,257,258,259},{260,261,262,263},{8,9,10,11},{12..., dimensions={0} | all-to-all | bytes 393216 | tf_op jit(solution)/shard_map/all_to_all | solution.py:260
  41.7 0.0 copy-start
  41.7 0.0 copy-start.1
  41.8 27.6 %all_to_all.22 = f32[4,12,8,128]{3,2,1,0:T(8,128)S(1)} all-to-all(f32[4,12,8,128]{3,2,1,0:T(8,128)S(1)} %broadcast_in_dim.10), channel_id=1, replica_groups={{0,4,256,260},{1,5,257,261},{2,6,258,262},{3,7,259,263},{8,12,264,268},..., dimensions={0} | all-to-all | bytes 393216 | tf_op jit(solution)/shard_map/all_to_all | solution.py:260
  69.4 0.1 broadcast_in_dim.11
  69.5 14.0 %all_to_all.23.mine = f32[16,12,8,128]{3,2,1,0:T(8,128)S(1)} all-to-all(f32[16,12,8,128]{3,2,1,0:T(8,128)S(1)} %broadcast_in_dim.11), channel_id=1, replica_groups=mesh['z_hi'=2,'y'=4,'x'=4,'core'=2,'z_lo'=8] {'y','x'}, dimensions={0} | all-to-all | bytes 1572864 | tf_op jit(solution)/shard_map/all_to_all | solution.py:261
  83.5 6.8 %collective-permute-start.1 = (f32[16,12,8,128]{3,2,1,0:T(8,128)S(1)}, f32[16,12,8,128]{3,2,1,0:T(8,128)S(1)}, u32[]{:S(2)}, u32[]{:S(2)}) collective-permute-start(f32[16,12,8,128]{3,2,1,0:T(8,128)S(1)} %all_to_all.23.mine), channel_id=1, source_target_pairs={{0,8},{8,0},{1,9},{9,1},{2,10},{10,2},{3,11},{11,3},{4,12},{12,4},... | collective-permute-start | bytes 2359304 | tf_op jit(solution)/shard_map/ppermute | solution.py:262
  90.3 1.7 %collective-permute-done.1.other = f32[16,12,8,128]{3,2,1,0:T(8,128)S(1)} collective-permute-done((f32[16,12,8,128]{3,2,1,0:T(8,128)S(1)}, f32[16,12,8,128]{3,2,1,0:T(8,128)S(1)}, u32[]{:S(2)}, u32[]{:S(2)}) %collective-permute-start.1) | collective-permute-done | bytes 786464 | tf_op jit(solution)/shard_map/ppermute | solution.py:262
  92.0 0.0 copy-done
  92.0 0.0 copy-done.1
  92.1 17.6 %shard_map.38 = f32[2,896,256]{2,1,0:T(8,128)} custom-call(f32[16,12,8,128]{3,2,1,0:T(8,128)S(1)} %all_to_all.23.mine, f32[16,12,8,128]{3,2,1,0:T(8,128)S(1)} %collective-permute-done.1.other, f32[896,384]{1,0:T(8,128)S(1)} %copy-done.1, f32[2,896,256]{2,1,0:T(8,128)S(1)} %copy-done), custom_call_target="tpu_custom_call" | custom-call | tf_op jit(solution)/shard_map/pallas_call | solution.py:240
  (5 shorter events, 0.1 us)
Async XLA Ops:
  3.9 11.1 %collective-permute-start = (f32[16,12,8,128]{3,2,1,0:T(8,128)}, f32[16,12,8,128]{3,2,1,0:T(8,128)S(1)}, u32[]{:S(2)}, u32[]{:S(2)}) collective-permute-start(f32[16,12,8,128]{3,2,1,0:T(8,128)} %get-tuple-element.8), channel_id=1, source_target_pairs={{0,8},{8,0},{1,9},{9,1},{2,10},{10,2},{3,11},{11,3},{4,12},{12,4},... | collective-permute-start | bytes 2359304 | tf_op jit(solution)/shard_map/ppermute | solution.py:256
  41.7 50.3 %copy-start = (f32[2,896,256]{2,1,0:T(8,128)S(1)}, f32[2,896,256]{2,1,0:T(8,128)}, u32[]{:S(2)}) copy-start(f32[2,896,256]{2,1,0:T(8,128)} %raw.3) | copy-start | bytes 5505028
  41.7 50.3 %copy-start.1 = (f32[896,384]{1,0:T(8,128)S(1)}, f32[896,384]{1,0:T(8,128)}, u32[]{:S(2)}) copy-start(f32[896,384]{1,0:T(8,128)} %prior.3) | copy-start | bytes 4128772
  83.5 8.6 %collective-permute-start.1 = (f32[16,12,8,128]{3,2,1,0:T(8,128)S(1)}, f32[16,12,8,128]{3,2,1,0:T(8,128)S(1)}, u32[]{:S(2)}, u32[]{:S(2)}) collective-permute-start(f32[16,12,8,128]{3,2,1,0:T(8,128)S(1)} %all_to_all.23.mine), channel_id=1, source_target_pairs={{0,8},{8,0},{1,9},{9,1},{2,10},{10,2},{3,11},{11,3},{4,12},{12,4},... | collective-permute-start | bytes 2359304 | tf_op jit(solution)/shard_map/ppermute | solution.py:262

commit v4 on v3

--- a/solution.py
+++ b/solution.py
@@ -13,7 +13,7 @@
 AXES = ("z_hi", "y", "x", "core", "z_lo")
 TILE = (8, 128)
 VMEM_LIMIT = 48 * 1024 * 1024
-PACK_VMEM_LIMIT = 60 * 1024 * 1024
+PACK_VMEM_LIMIT = 56 * 1024 * 1024
 
 
 def dot(left, right, left_dim=1, right_dim=0):
@@ -82,7 +82,7 @@
 
 
 def pack(pivot_rows, prior, raw, groups):
-    shape = jax.ShapeDtypeStruct((groups, 12) + TILE, F32)
+    shape = pltpu.VMEM((groups, 12) + TILE, F32)
     vmem, smem = pl.BlockSpec(memory_space=pltpu.VMEM), pl.BlockSpec(memory_space=pltpu.SMEM)
     where_it_is = pl.BlockSpec(memory_space=pl.ANY)
     return pl.pallas_call(
@@ -175,7 +175,7 @@
     return jnp.concatenate(finished, axis=0)
 
 
-def steps_kernel(mine, other, prior, raw, out, packed):
+def steps_kernel(mine, other, prior, raw, result, packed, out, sems):
     core = lax.axis_index("core")
     half = mine.shape[0]
     packed[pl.ds(core * half, half)] = mine[...]
@@ -187,6 +187,7 @@
 
     prior_0, prior_1 = columns(0, 3), columns(5, 3)
     rows_here = prior.shape[0]
+    copies = []
     chunks = [slice(rows_here * c // 4, rows_here * (c + 1) // 4) for c in range(4)]
 
     def symmetrized(block):
@@ -197,6 +198,8 @@
 
     def finish(step, inverse, rows):
         out[step, rows] = dot(out[step, rows], inverse, 1, 1)
+        copies.append(pltpu.make_async_copy(out.at[step, rows], result.at[step, rows], sems.at[len(copies)]))
+        copies[-1].start()
 
     def take(pivots, rows):
         out[1, rows] = out[1, rows] - dot(out[0, rows], pivots, 1, 1)
@@ -218,13 +221,13 @@
         later["cross"] = columns(8, 2) - dot(prior_1, prior_0, 1, 1)
 
     def block():
-        later["block"] = symmetrized(columns(10, 2) - dot(prior_1, prior_1, 1, 1))
+        later["block"] = symmetrized(columns(10, 2)) - dot(prior_1, prior_1, 1, 1)
 
     tasks.insert(0, cross)
     tasks.insert(0, block)
-    inverse_0 = cholesky_inverse(symmetrized(columns(3, 2) - dot(prior_0, prior_0, 1, 1)), beside(tasks))
+    inverse_0 = cholesky_inverse(symmetrized(columns(3, 2)) - dot(prior_0, prior_0, 1, 1), beside(tasks))
     fresh_pivots = dot(later["cross"], inverse_0, 1, 1)
-    block_1 = later["block"] - symmetrized(dot(fresh_pivots, fresh_pivots, 1, 1))
+    block_1 = later["block"] - dot(fresh_pivots, fresh_pivots, 1, 1)
     tasks += [functools.partial(finish, 0, inverse_0, rows) for rows in chunks]
     tasks += [functools.partial(take, fresh_pivots, rows) for rows in chunks]
     inverse_1 = cholesky_inverse(block_1, beside(tasks))
@@ -232,6 +235,8 @@
         task()
     for rows in chunks:
         finish(1, inverse_1, rows)
+    for copy in copies:
+        copy.wait()
 
 
 def steps(mine, other, prior, raw):
@@ -241,8 +246,12 @@
         steps_kernel,
         out_shape=jax.ShapeDtypeStruct(raw.shape, F32),
         in_specs=[vmem] * 4,
-        out_specs=vmem,
-        scratch_shapes=[pltpu.VMEM((2 * groups, 12) + TILE, F32)],
+        out_specs=pl.BlockSpec(memory_space=pl.ANY),
+        scratch_shapes=[
+            pltpu.VMEM((2 * groups, 12) + TILE, F32),
+            pltpu.VMEM(raw.shape, F32),
+            pltpu.SemaphoreType.DMA((8,)),
+        ],
         compiler_params=pltpu.CompilerParams(vmem_limit_bytes=VMEM_LIMIT),
     )(mine, other, prior, raw)
 

time: 110 us -> 108 us (0.982)
  Pallas kernels: 21.5 us -> 18.8 us
  other arithmetic: 1.29 us -> 0.16 us
    pallas_call x1, Pallas kernels: 3.89 us -> 1.74 us  [pack(): pl.pallas_call(pack_kernel, out_shape=(shape, shape), in_specs=[smem, whe...]
    add x1, other arithmetic: 1.22 us -> 0.09 us  [body(): total = keep + lax.ppermute(send, 'core', swap)]
where the time goes in v4:
time: 108 us; the launch traced here: 107 us
  blocking collectives  67.5 us (62%)
  Pallas kernels  18.8 us (17%)
  starting transfers between devices  16.9 us (16%)
  waiting for transfers between devices  3.6 us (3%)
    all_to_all x2, blocking collectives, body(): lax.all_to_all(copies, line, 0, 0, axis_index_groups=groups)  36.9 us
    pallas_call x1, Pallas kernels, steps(): pl.pallas_call(steps_kernel, out_shape=jax.ShapeDtypeStruct(raw.shape, F3...  17.1 us
    all_to_all x1, blocking collectives, body(): total = jnp.sum(lax.all_to_all(total, plane, 0, 0), axis=0)  16.7 us
    all_to_all x1, blocking collectives, body(): lax.all_to_all(jnp.broadcast_to(total, (in_plane,) + total.shape), plane,...  13.8 us
    ppermute x1, starting transfers between devices, body(): total = keep + lax.ppermute(send, 'core', swap)  10 us
    ppermute x1, starting transfers between devices, body(): other = lax.ppermute(mine, 'core', swap)  6.84 us
  transfers between devices with their start and end apart: 2, of which 2 were waited for; matrix products, arithmetic and copies ran while one was open for 0% of the time, Pallas kernels for 0%

profile of v4, /device:TPU:1, one launch (start us, length us, event | category | flops | bytes accessed | tf_op | source)
XLA Modules:
  0.0 107.3 jit_solution(2344246366278099479)
XLA Ops:
  0.0 1.7 %shard_map.37 = (f32[16,12,8,128]{3,2,1,0:T(8,128)S(1)}, f32[16,12,8,128]{3,2,1,0:T(8,128)S(1)}) custom-call(s32[2,256]{1,0:T(2,128)} %pivots.1, f32[896,384]{1,0:T(8,128)} %prior.3, f32[2,896,256]{2,1,0:T(8,128)} %raw.3), custom_call_target="tpu_custom_call" | custom-call | tf_op jit(solution)/shard_map/pallas_call | solution.py:88
  1.8 10.0 %collective-permute-start = (f32[16,12,8,128]{3,2,1,0:T(8,128)S(1)}, f32[16,12,8,128]{3,2,1,0:T(8,128)S(1)}, u32[]{:S(2)}, u32[]{:S(2)}) collective-permute-start(f32[16,12,8,128]{3,2,1,0:T(8,128)S(1)} %get-tuple-element.8), channel_id=1, source_target_pairs={{0,8},{8,0},{1,9},{9,1},{2,10},{10,2},{3,11},{11,3},{4,12},{12,4},... | collective-permute-start | bytes 2359304 | tf_op jit(solution)/shard_map/ppermute | solution.py:265
  11.8 1.9 %collective-permute-done = f32[16,12,8,128]{3,2,1,0:T(8,128)S(1)} collective-permute-done((f32[16,12,8,128]{3,2,1,0:T(8,128)S(1)}, f32[16,12,8,128]{3,2,1,0:T(8,128)S(1)}, u32[]{:S(2)}, u32[]{:S(2)}) %collective-permute-start) | collective-permute-done | bytes 786464 | tf_op jit(solution)/shard_map/ppermute | solution.py:265
  13.7 0.1 add.3
  13.8 16.7 %all_to_all.20 = f32[16,12,8,128]{3,2,1,0:T(8,128)S(1)} all-to-all(f32[16,12,8,128]{3,2,1,0:T(8,128)S(1)} %add.3), channel_id=1, replica_groups=mesh['z_hi'=2,'y'=4,'x'=4,'core'=2,'z_lo'=8] {'y','x'}, dimensions={0} | all-to-all | bytes 1572864 | tf_op jit(solution)/shard_map/all_to_all | solution.py:266
  30.5 9.0 %all_to_all.21 = f32[4,12,8,128]{3,2,1,0:T(8,128)S(1)} all-to-all(f32[4,12,8,128]{3,2,1,0:T(8,128)S(1)} %broadcast_in_dim.9), channel_id=1, replica_groups={{0,1,2,3},{4,5,6,7},{256,257,258,259},{260,261,262,263},{8,9,10,11},{12..., dimensions={0} | all-to-all | bytes 393216 | tf_op jit(solution)/shard_map/all_to_all | solution.py:269
  39.5 0.0 copy-start
  39.5 0.0 copy-start.1
  39.6 27.9 %all_to_all.22 = f32[4,12,8,128]{3,2,1,0:T(8,128)S(1)} all-to-all(f32[4,12,8,128]{3,2,1,0:T(8,128)S(1)} %broadcast_in_dim.10), channel_id=1, replica_groups={{0,4,256,260},{1,5,257,261},{2,6,258,262},{3,7,259,263},{8,12,264,268},..., dimensions={0} | all-to-all | bytes 393216 | tf_op jit(solution)/shard_map/all_to_all | solution.py:269
  67.5 0.1 broadcast_in_dim.11
  67.6 13.8 %all_to_all.23.mine = f32[16,12,8,128]{3,2,1,0:T(8,128)S(1)} all-to-all(f32[16,12,8,128]{3,2,1,0:T(8,128)S(1)} %broadcast_in_dim.11), channel_id=1, replica_groups=mesh['z_hi'=2,'y'=4,'x'=4,'core'=2,'z_lo'=8] {'y','x'}, dimensions={0} | all-to-all | bytes 1572864 | tf_op jit(solution)/shard_map/all_to_all | solution.py:270
  81.4 6.8 %collective-permute-start.1 = (f32[16,12,8,128]{3,2,1,0:T(8,128)S(1)}, f32[16,12,8,128]{3,2,1,0:T(8,128)S(1)}, u32[]{:S(2)}, u32[]{:S(2)}) collective-permute-start(f32[16,12,8,128]{3,2,1,0:T(8,128)S(1)} %all_to_all.23.mine), channel_id=1, source_target_pairs={{0,8},{8,0},{1,9},{9,1},{2,10},{10,2},{3,11},{11,3},{4,12},{12,4},... | collective-permute-start | bytes 2359304 | tf_op jit(solution)/shard_map/ppermute | solution.py:271
  88.3 1.7 %collective-permute-done.1.other = f32[16,12,8,128]{3,2,1,0:T(8,128)S(1)} collective-permute-done((f32[16,12,8,128]{3,2,1,0:T(8,128)S(1)}, f32[16,12,8,128]{3,2,1,0:T(8,128)S(1)}, u32[]{:S(2)}, u32[]{:S(2)}) %collective-permute-start.1) | collective-permute-done | bytes 786464 | tf_op jit(solution)/shard_map/ppermute | solution.py:271
  90.0 0.0 copy-done
  90.0 0.0 copy-done.1
  90.0 17.1 %shard_map.38 = f32[2,896,256]{2,1,0:T(8,128)} custom-call(f32[16,12,8,128]{3,2,1,0:T(8,128)S(1)} %all_to_all.23.mine, f32[16,12,8,128]{3,2,1,0:T(8,128)S(1)} %collective-permute-done.1.other, f32[896,384]{1,0:T(8,128)S(1)} %copy-done.1, f32[2,896,256]{2,1,0:T(8,128)S(1)} %copy-done), custom_call_target="tpu_custom_call" | custom-call | tf_op jit(solution)/shard_map/pallas_call | solution.py:245
  (5 shorter events, 0.1 us)
Async XLA Ops:
  1.8 11.9 %collective-permute-start = (f32[16,12,8,128]{3,2,1,0:T(8,128)S(1)}, f32[16,12,8,128]{3,2,1,0:T(8,128)S(1)}, u32[]{:S(2)}, u32[]{:S(2)}) collective-permute-start(f32[16,12,8,128]{3,2,1,0:T(8,128)S(1)} %get-tuple-element.8), channel_id=1, source_target_pairs={{0,8},{8,0},{1,9},{9,1},{2,10},{10,2},{3,11},{11,3},{4,12},{12,4},... | collective-permute-start | bytes 2359304 | tf_op jit(solution)/shard_map/ppermute | solution.py:265
  39.5 50.5 %copy-start = (f32[2,896,256]{2,1,0:T(8,128)S(1)}, f32[2,896,256]{2,1,0:T(8,128)}, u32[]{:S(2)}) copy-start(f32[2,896,256]{2,1,0:T(8,128)} %raw.3) | copy-start | bytes 5505028
  39.5 50.5 %copy-start.1 = (f32[896,384]{1,0:T(8,128)S(1)}, f32[896,384]{1,0:T(8,128)}, u32[]{:S(2)}) copy-start(f32[896,384]{1,0:T(8,128)} %prior.3) | copy-start | bytes 4128772
  81.4 8.6 %collective-permute-start.1 = (f32[16,12,8,128]{3,2,1,0:T(8,128)S(1)}, f32[16,12,8,128]{3,2,1,0:T(8,128)S(1)}, u32[]{:S(2)}, u32[]{:S(2)}) collective-permute-start(f32[16,12,8,128]{3,2,1,0:T(8,128)S(1)} %all_to_all.23.mine), channel_id=1, source_target_pairs={{0,8},{8,0},{1,9},{9,1},{2,10},{10,2},{3,11},{11,3},{4,12},{12,4},... | collective-permute-start | bytes 2359304 | tf_op jit(solution)/shard_map/ppermute | solution.py:271

commit v5 on v4

--- a/solution.py
+++ b/solution.py
@@ -147,30 +147,40 @@
     return jnp.concatenate(done, axis=0)
 
 
-def cholesky_inverse(symmetric, beside):
-    size, width = symmetric.shape[0], 64
-    work = symmetric
-    finished = []
+def cholesky_inverse(first, whole, beside):
+    width, size = first.shape[0], 4 * first.shape[0]
+    finished, made = [], []
     for which in range(size // width):
         low, high = which * width, (which + 1) * width
         at = low % 128
         rest = size - high
+        urgent = [whole]
+
+        def call(urgent=urgent):
+            if urgent:
+                made.append(urgent.pop()())
+            else:
+                beside()
+
+        inverse = eliminate(first, at, call)
+        work = made[-1]
         block_of = lax.broadcasted_iota(jnp.int32, (width, size), 1) // width
         on_diagonal = lax.broadcasted_iota(jnp.int32, (width, size), 1) == lax.broadcasted_iota(jnp.int32, (width, size), 0) + low
         line = jnp.where(block_of == which, on_diagonal.astype(F32), work[:width])
         blank = jnp.zeros_like(line)
-        line = jnp.concatenate([blank, line] if at == 0 else [line, blank], axis=0)
-        inverse = eliminate(work[:width, low:high], at, beside)
+        line = dot(inverse, jnp.concatenate([blank, line] if at == 0 else [line, blank], axis=0))
         if rest:
             column = work[width:, low:high]
             blank = jnp.zeros_like(column)
             column = jnp.concatenate([blank, column] if at == 0 else [column, blank], axis=1)
-            factor = dot(column, inverse, 1, 1)
-            block_of_rest = lax.broadcasted_iota(jnp.int32, (rest, size), 1) // width
-            work = jnp.where(block_of_rest == which, 0.0, work[width:])
-        line = dot(inverse, line)
-        if rest:
-            work = work - dot(factor, line)
+            tile = slice(high // 128 * 128, high // 128 * 128 + 128)
+            near = work[width : 2 * width, tile] - dot(dot(column[:width], inverse, 1, 1), line[:, tile])
+            first = near[:, high % 128 : high % 128 + width]
+
+            def whole(work=work, column=column, inverse=inverse, line=line, which=which, rest=rest):
+                block_of = lax.broadcasted_iota(jnp.int32, (rest, size), 1) // width
+                return jnp.where(block_of == which, 0.0, work[width:]) - dot(dot(column, inverse, 1, 1), line)
+
         finished.append(jnp.where(block_of <= which, line, 0.0))
     return jnp.concatenate(finished, axis=0)
 
@@ -201,14 +211,14 @@
         copies.append(pltpu.make_async_copy(out.at[step, rows], result.at[step, rows], sems.at[len(copies)]))
         copies[-1].start()
 
-    def take(pivots, rows):
-        out[1, rows] = out[1, rows] - dot(out[0, rows], pivots, 1, 1)
+    def take(rows):
+        out[1, rows] = out[1, rows] - dot(out[0, rows], later["fresh"], 1, 1)
 
     def beside(tasks):
         calls = iter(range(1000))
 
         def call():
-            if next(calls) % 3 == 0 and tasks:
+            if next(calls) % 7 in (2, 4, 5) and tasks:
                 tasks.pop(0)()
 
         return call
@@ -225,12 +235,22 @@
 
     tasks.insert(0, cross)
     tasks.insert(0, block)
-    inverse_0 = cholesky_inverse(symmetrized(columns(3, 2)) - dot(prior_0, prior_0, 1, 1), beside(tasks))
-    fresh_pivots = dot(later["cross"], inverse_0, 1, 1)
-    block_1 = later["block"] - dot(fresh_pivots, fresh_pivots, 1, 1)
+    raw_block = columns(3, 2)
+    lead = slice(0, 64)
+    inverse_0 = cholesky_inverse(
+        symmetrized(raw_block[lead, lead]) - dot(prior_0[lead], prior_0[lead], 1, 1),
+        lambda: symmetrized(raw_block) - dot(prior_0, prior_0, 1, 1),
+        beside(tasks),
+    )
+    lead_pivots = dot(later["cross"][lead], inverse_0, 1, 1)
+
+    def block_1():
+        later["fresh"] = dot(later["cross"], inverse_0, 1, 1)
+        return later["block"] - dot(later["fresh"], later["fresh"], 1, 1)
+
     tasks += [functools.partial(finish, 0, inverse_0, rows) for rows in chunks]
-    tasks += [functools.partial(take, fresh_pivots, rows) for rows in chunks]
-    inverse_1 = cholesky_inverse(block_1, beside(tasks))
+    tasks += [functools.partial(take, rows) for rows in chunks]
+    inverse_1 = cholesky_inverse(later["block"][lead, lead] - dot(lead_pivots, lead_pivots, 1, 1), block_1, beside(tasks))
     for task in tasks:
         task()
     for rows in chunks:

time: 108 us -> 106 us (0.981)
  Pallas kernels: 18.8 us -> 17.7 us
    pallas_call x1, Pallas kernels: 17.1 us -> 15.7 us  [steps(): pl.pallas_call(steps_kernel, out_shape=jax.ShapeDtypeStruct(raw.shape, F3...]
    ppermute x1, starting transfers between devices: 10 us -> 8.68 us  [body(): total = keep + lax.ppermute(send, 'core', swap)]
where the time goes in v5:
time: 106 us; the launch traced here: 105 us
  blocking collectives  67.6 us (64%)
  Pallas kernels  17.7 us (17%)
  starting transfers between devices  15.9 us (15%)
  waiting for transfers between devices  3.6 us (3%)
    all_to_all x2, blocking collectives, body(): lax.all_to_all(copies, line, 0, 0, axis_index_groups=groups)  37.1 us
    all_to_all x1, blocking collectives, body(): total = jnp.sum(lax.all_to_all(total, plane, 0, 0), axis=0)  16.7 us
    pallas_call x1, Pallas kernels, steps(): pl.pallas_call(steps_kernel, out_shape=jax.ShapeDtypeStruct(raw.shape, F3...  15.7 us
    all_to_all x1, blocking collectives, body(): lax.all_to_all(jnp.broadcast_to(total, (in_plane,) + total.shape), plane,...  13.8 us
    ppermute x1, starting transfers between devices, body(): total = keep + lax.ppermute(send, 'core', swap)  8.68 us
    ppermute x1, starting transfers between devices, body(): other = lax.ppermute(mine, 'core', swap)  7.26 us
  transfers between devices with their start and end apart: 2, of which 2 were waited for; matrix products, arithmetic and copies ran while one was open for 0% of the time, Pallas kernels for 0%

profile of v5, /device:TPU:1, one launch (start us, length us, event | category | flops | bytes accessed | tf_op | source)
XLA Modules:
  0.0 105.3 jit_solution(6749663018263940870)
XLA Ops:
  0.0 2.0 %shard_map.37 = (f32[16,12,8,128]{3,2,1,0:T(8,128)S(1)}, f32[16,12,8,128]{3,2,1,0:T(8,128)S(1)}) custom-call(s32[2,256]{1,0:T(2,128)} %pivots.1, f32[896,384]{1,0:T(8,128)} %prior.3, f32[2,896,256]{2,1,0:T(8,128)} %raw.3), custom_call_target="tpu_custom_call" | custom-call | tf_op jit(solution)/shard_map/pallas_call | solution.py:88
  2.0 8.7 %collective-permute-start = (f32[16,12,8,128]{3,2,1,0:T(8,128)S(1)}, f32[16,12,8,128]{3,2,1,0:T(8,128)S(1)}, u32[]{:S(2)}, u32[]{:S(2)}) collective-permute-start(f32[16,12,8,128]{3,2,1,0:T(8,128)S(1)} %get-tuple-element.8), channel_id=1, source_target_pairs={{0,8},{8,0},{1,9},{9,1},{2,10},{10,2},{3,11},{11,3},{4,12},{12,4},... | collective-permute-start | bytes 2359304 | tf_op jit(solution)/shard_map/ppermute | solution.py:285
  10.7 1.9 %collective-permute-done = f32[16,12,8,128]{3,2,1,0:T(8,128)S(1)} collective-permute-done((f32[16,12,8,128]{3,2,1,0:T(8,128)S(1)}, f32[16,12,8,128]{3,2,1,0:T(8,128)S(1)}, u32[]{:S(2)}, u32[]{:S(2)}) %collective-permute-start) | collective-permute-done | bytes 786464 | tf_op jit(solution)/shard_map/ppermute | solution.py:285
  12.6 0.1 add.3
  12.7 16.7 %all_to_all.20 = f32[16,12,8,128]{3,2,1,0:T(8,128)S(1)} all-to-all(f32[16,12,8,128]{3,2,1,0:T(8,128)S(1)} %add.3), channel_id=1, replica_groups=mesh['z_hi'=2,'y'=4,'x'=4,'core'=2,'z_lo'=8] {'y','x'}, dimensions={0} | all-to-all | bytes 1572864 | tf_op jit(solution)/shard_map/all_to_all | solution.py:286
  29.4 9.5 %all_to_all.21 = f32[4,12,8,128]{3,2,1,0:T(8,128)S(1)} all-to-all(f32[4,12,8,128]{3,2,1,0:T(8,128)S(1)} %broadcast_in_dim.9), channel_id=1, replica_groups={{0,1,2,3},{4,5,6,7},{256,257,258,259},{260,261,262,263},{8,9,10,11},{12..., dimensions={0} | all-to-all | bytes 393216 | tf_op jit(solution)/shard_map/all_to_all | solution.py:289
  39.0 0.0 copy-start
  39.0 0.0 copy-start.1
  39.0 27.6 %all_to_all.22 = f32[4,12,8,128]{3,2,1,0:T(8,128)S(1)} all-to-all(f32[4,12,8,128]{3,2,1,0:T(8,128)S(1)} %broadcast_in_dim.10), channel_id=1, replica_groups={{0,4,256,260},{1,5,257,261},{2,6,258,262},{3,7,259,263},{8,12,264,268},..., dimensions={0} | all-to-all | bytes 393216 | tf_op jit(solution)/shard_map/all_to_all | solution.py:289
  66.6 0.1 broadcast_in_dim.11
  66.7 13.8 %all_to_all.23.mine = f32[16,12,8,128]{3,2,1,0:T(8,128)S(1)} all-to-all(f32[16,12,8,128]{3,2,1,0:T(8,128)S(1)} %broadcast_in_dim.11), channel_id=1, replica_groups=mesh['z_hi'=2,'y'=4,'x'=4,'core'=2,'z_lo'=8] {'y','x'}, dimensions={0} | all-to-all | bytes 1572864 | tf_op jit(solution)/shard_map/all_to_all | solution.py:290
  80.5 7.3 %collective-permute-start.1 = (f32[16,12,8,128]{3,2,1,0:T(8,128)S(1)}, f32[16,12,8,128]{3,2,1,0:T(8,128)S(1)}, u32[]{:S(2)}, u32[]{:S(2)}) collective-permute-start(f32[16,12,8,128]{3,2,1,0:T(8,128)S(1)} %all_to_all.23.mine), channel_id=1, source_target_pairs={{0,8},{8,0},{1,9},{9,1},{2,10},{10,2},{3,11},{11,3},{4,12},{12,4},... | collective-permute-start | bytes 2359304 | tf_op jit(solution)/shard_map/ppermute | solution.py:291
  87.7 1.7 %collective-permute-done.1.other = f32[16,12,8,128]{3,2,1,0:T(8,128)S(1)} collective-permute-done((f32[16,12,8,128]{3,2,1,0:T(8,128)S(1)}, f32[16,12,8,128]{3,2,1,0:T(8,128)S(1)}, u32[]{:S(2)}, u32[]{:S(2)}) %collective-permute-start.1) | collective-permute-done | bytes 786464 | tf_op jit(solution)/shard_map/ppermute | solution.py:291
  89.4 0.0 copy-done
  89.5 0.0 copy-done.1
  89.5 15.7 %shard_map.38 = f32[2,896,256]{2,1,0:T(8,128)} custom-call(f32[16,12,8,128]{3,2,1,0:T(8,128)S(1)} %all_to_all.23.mine, f32[16,12,8,128]{3,2,1,0:T(8,128)S(1)} %collective-permute-done.1.other, f32[896,384]{1,0:T(8,128)S(1)} %copy-done.1, f32[2,896,256]{2,1,0:T(8,128)S(1)} %copy-done), custom_call_target="tpu_custom_call" | custom-call | tf_op jit(solution)/shard_map/pallas_call | solution.py:265
  (5 shorter events, 0.1 us)
Async XLA Ops:
  2.0 10.6 %collective-permute-start = (f32[16,12,8,128]{3,2,1,0:T(8,128)S(1)}, f32[16,12,8,128]{3,2,1,0:T(8,128)S(1)}, u32[]{:S(2)}, u32[]{:S(2)}) collective-permute-start(f32[16,12,8,128]{3,2,1,0:T(8,128)S(1)} %get-tuple-element.8), channel_id=1, source_target_pairs={{0,8},{8,0},{1,9},{9,1},{2,10},{10,2},{3,11},{11,3},{4,12},{12,4},... | collective-permute-start | bytes 2359304 | tf_op jit(solution)/shard_map/ppermute | solution.py:285
  39.0 50.5 %copy-start = (f32[2,896,256]{2,1,0:T(8,128)S(1)}, f32[2,896,256]{2,1,0:T(8,128)}, u32[]{:S(2)}) copy-start(f32[2,896,256]{2,1,0:T(8,128)} %raw.3) | copy-start | bytes 5505028
  39.0 50.5 %copy-start.1 = (f32[896,384]{1,0:T(8,128)S(1)}, f32[896,384]{1,0:T(8,128)}, u32[]{:S(2)}) copy-start(f32[896,384]{1,0:T(8,128)} %prior.3) | copy-start | bytes 4128772
  80.5 9.0 %collective-permute-start.1 = (f32[16,12,8,128]{3,2,1,0:T(8,128)S(1)}, f32[16,12,8,128]{3,2,1,0:T(8,128)S(1)}, u32[]{:S(2)}, u32[]{:S(2)}) collective-permute-start(f32[16,12,8,128]{3,2,1,0:T(8,128)S(1)} %all_to_all.23.mine), channel_id=1, source_target_pairs={{0,8},{8,0},{1,9},{9,1},{2,10},{10,2},{3,11},{11,3},{4,12},{12,4},... | collective-permute-start | bytes 2359304 | tf_op jit(solution)/shard_map/ppermute | solution.py:291

commit v6 on v5

--- a/solution.py
+++ b/solution.py
@@ -284,7 +284,7 @@
     keep, send = pack(pivot_rows, prior, raw, in_plane)
     total = keep + lax.ppermute(send, "core", swap)
     total = jnp.sum(lax.all_to_all(total, plane, 0, 0), axis=0)
-    for groups in ([[4 * run + k for k in range(4)] for run in range(4)], [[4 * run + k for run in range(4)] for k in range(4)]):
+    for groups in ([[4 * run + k for run in range(4)] for k in range(4)], [[4 * run + k for k in range(4)] for run in range(4)]):
         copies = jnp.broadcast_to(total, (4,) + total.shape)
         total = jnp.sum(lax.all_to_all(copies, line, 0, 0, axis_index_groups=groups), axis=0)
     mine = lax.all_to_all(jnp.broadcast_to(total, (in_plane,) + total.shape), plane, 0, 0)

time: 106 us -> 108 us (1.019)
  blocking collectives: 67.6 us -> 69.4 us
    all_to_all x2, blocking collectives: 37.1 us -> 39 us  [body(): lax.all_to_all(copies, line, 0, 0, axis_index_groups=groups)]
where the time goes in v6:
time: 108 us; the launch traced here: 107 us
  blocking collectives  69.4 us (64%)
  Pallas kernels  18.2 us (17%)
  starting transfers between devices  15.5 us (14%)
  waiting for transfers between devices  3.6 us (3%)
    all_to_all x2, blocking collectives, body(): lax.all_to_all(copies, line, 0, 0, axis_index_groups=groups)  39 us
    all_to_all x1, blocking collectives, body(): total = jnp.sum(lax.all_to_all(total, plane, 0, 0), axis=0)  16.7 us
    pallas_call x1, Pallas kernels, steps(): pl.pallas_call(steps_kernel, out_shape=jax.ShapeDtypeStruct(raw.shape, F3...  15.7 us
    all_to_all x1, blocking collectives, body(): lax.all_to_all(jnp.broadcast_to(total, (in_plane,) + total.shape), plane,...  13.7 us
    ppermute x1, starting transfers between devices, body(): total = keep + lax.ppermute(send, 'core', swap)  8.11 us
    ppermute x1, starting transfers between devices, body(): other = lax.ppermute(mine, 'core', swap)  7.41 us
    pallas_call x1, Pallas kernels, pack(): pl.pallas_call(pack_kernel, out_shape=(shape, shape), in_specs=[smem, whe...  2.57 us
  transfers between devices with their start and end apart: 2, of which 2 were waited for; matrix products, arithmetic and copies ran while one was open for 0% of the time, Pallas kernels for 0%

profile of v6, /device:TPU:1, one launch (start us, length us, event | category | flops | bytes accessed | tf_op | source)
XLA Modules:
  0.0 107.3 jit_solution(2361786053818815160)
XLA Ops:
  0.0 2.6 %shard_map.37 = (f32[16,12,8,128]{3,2,1,0:T(8,128)S(1)}, f32[16,12,8,128]{3,2,1,0:T(8,128)S(1)}) custom-call(s32[2,256]{1,0:T(2,128)} %pivots.1, f32[896,384]{1,0:T(8,128)} %prior.3, f32[2,896,256]{2,1,0:T(8,128)} %raw.3), custom_call_target="tpu_custom_call" | custom-call | tf_op jit(solution)/shard_map/pallas_call | solution.py:88
  2.6 8.1 %collective-permute-start = (f32[16,12,8,128]{3,2,1,0:T(8,128)S(1)}, f32[16,12,8,128]{3,2,1,0:T(8,128)S(1)}, u32[]{:S(2)}, u32[]{:S(2)}) collective-permute-start(f32[16,12,8,128]{3,2,1,0:T(8,128)S(1)} %get-tuple-element.8), channel_id=1, source_target_pairs={{0,8},{8,0},{1,9},{9,1},{2,10},{10,2},{3,11},{11,3},{4,12},{12,4},... | collective-permute-start | bytes 2359304 | tf_op jit(solution)/shard_map/ppermute | solution.py:285
  10.7 1.9 %collective-permute-done = f32[16,12,8,128]{3,2,1,0:T(8,128)S(1)} collective-permute-done((f32[16,12,8,128]{3,2,1,0:T(8,128)S(1)}, f32[16,12,8,128]{3,2,1,0:T(8,128)S(1)}, u32[]{:S(2)}, u32[]{:S(2)}) %collective-permute-start) | collective-permute-done | bytes 786464 | tf_op jit(solution)/shard_map/ppermute | solution.py:285
  12.6 0.1 add.3
  12.7 16.7 %all_to_all.20 = f32[16,12,8,128]{3,2,1,0:T(8,128)S(1)} all-to-all(f32[16,12,8,128]{3,2,1,0:T(8,128)S(1)} %add.3), channel_id=1, replica_groups=mesh['z_hi'=2,'y'=4,'x'=4,'core'=2,'z_lo'=8] {'y','x'}, dimensions={0} | all-to-all | bytes 1572864 | tf_op jit(solution)/shard_map/all_to_all | solution.py:286
  29.4 27.4 %all_to_all.21 = f32[4,12,8,128]{3,2,1,0:T(8,128)S(1)} all-to-all(f32[4,12,8,128]{3,2,1,0:T(8,128)S(1)} %broadcast_in_dim.9), channel_id=1, replica_groups={{0,4,256,260},{1,5,257,261},{2,6,258,262},{3,7,259,263},{8,12,264,268},..., dimensions={0} | all-to-all | bytes 393216 | tf_op jit(solution)/shard_map/all_to_all | solution.py:289
  56.8 0.0 copy-start
  56.8 0.0 copy-start.1
  56.9 11.6 %all_to_all.22 = f32[4,12,8,128]{3,2,1,0:T(8,128)S(1)} all-to-all(f32[4,12,8,128]{3,2,1,0:T(8,128)S(1)} %broadcast_in_dim.10), channel_id=1, replica_groups={{0,1,2,3},{4,5,6,7},{256,257,258,259},{260,261,262,263},{8,9,10,11},{12..., dimensions={0} | all-to-all | bytes 393216 | tf_op jit(solution)/shard_map/all_to_all | solution.py:289
  68.5 0.1 broadcast_in_dim.11
  68.6 13.7 %all_to_all.23.mine = f32[16,12,8,128]{3,2,1,0:T(8,128)S(1)} all-to-all(f32[16,12,8,128]{3,2,1,0:T(8,128)S(1)} %broadcast_in_dim.11), channel_id=1, replica_groups=mesh['z_hi'=2,'y'=4,'x'=4,'core'=2,'z_lo'=8] {'y','x'}, dimensions={0} | all-to-all | bytes 1572864 | tf_op jit(solution)/shard_map/all_to_all | solution.py:290
  82.3 7.4 %collective-permute-start.1 = (f32[16,12,8,128]{3,2,1,0:T(8,128)S(1)}, f32[16,12,8,128]{3,2,1,0:T(8,128)S(1)}, u32[]{:S(2)}, u32[]{:S(2)}) collective-permute-start(f32[16,12,8,128]{3,2,1,0:T(8,128)S(1)} %all_to_all.23.mine), channel_id=1, source_target_pairs={{0,8},{8,0},{1,9},{9,1},{2,10},{10,2},{3,11},{11,3},{4,12},{12,4},... | collective-permute-start | bytes 2359304 | tf_op jit(solution)/shard_map/ppermute | solution.py:291
  89.7 1.7 %collective-permute-done.1.other = f32[16,12,8,128]{3,2,1,0:T(8,128)S(1)} collective-permute-done((f32[16,12,8,128]{3,2,1,0:T(8,128)S(1)}, f32[16,12,8,128]{3,2,1,0:T(8,128)S(1)}, u32[]{:S(2)}, u32[]{:S(2)}) %collective-permute-start.1) | collective-permute-done | bytes 786464 | tf_op jit(solution)/shard_map/ppermute | solution.py:291
  91.4 0.0 copy-done
  91.4 0.0 copy-done.1
  91.4 15.7 %shard_map.38 = f32[2,896,256]{2,1,0:T(8,128)} custom-call(f32[16,12,8,128]{3,2,1,0:T(8,128)S(1)} %all_to_all.23.mine, f32[16,12,8,128]{3,2,1,0:T(8,128)S(1)} %collective-permute-done.1.other, f32[896,384]{1,0:T(8,128)S(1)} %copy-done.1, f32[2,896,256]{2,1,0:T(8,128)S(1)} %copy-done), custom_call_target="tpu_custom_call" | custom-call | tf_op jit(solution)/shard_map/pallas_call | solution.py:265
  (5 shorter events, 0.1 us)
Async XLA Ops:
  2.6 10.0 %collective-permute-start = (f32[16,12,8,128]{3,2,1,0:T(8,128)S(1)}, f32[16,12,8,128]{3,2,1,0:T(8,128)S(1)}, u32[]{:S(2)}, u32[]{:S(2)}) collective-permute-start(f32[16,12,8,128]{3,2,1,0:T(8,128)S(1)} %get-tuple-element.8), channel_id=1, source_target_pairs={{0,8},{8,0},{1,9},{9,1},{2,10},{10,2},{3,11},{11,3},{4,12},{12,4},... | collective-permute-start | bytes 2359304 | tf_op jit(solution)/shard_map/ppermute | solution.py:285
  56.8 34.6 %copy-start = (f32[2,896,256]{2,1,0:T(8,128)S(1)}, f32[2,896,256]{2,1,0:T(8,128)}, u32[]{:S(2)}) copy-start(f32[2,896,256]{2,1,0:T(8,128)} %raw.3) | copy-start | bytes 5505028
  56.8 34.6 %copy-start.1 = (f32[896,384]{1,0:T(8,128)S(1)}, f32[896,384]{1,0:T(8,128)}, u32[]{:S(2)}) copy-start(f32[896,384]{1,0:T(8,128)} %prior.3) | copy-start | bytes 4128772
  82.3 9.1 %collective-permute-start.1 = (f32[16,12,8,128]{3,2,1,0:T(8,128)S(1)}, f32[16,12,8,128]{3,2,1,0:T(8,128)S(1)}, u32[]{:S(2)}, u32[]{:S(2)}) collective-permute-start(f32[16,12,8,128]{3,2,1,0:T(8,128)S(1)} %all_to_all.23.mine), channel_id=1, source_target_pairs={{0,8},{8,0},{1,9},{9,1},{2,10},{10,2},{3,11},{11,3},{4,12},{12,4},... | collective-permute-start | bytes 2359304 | tf_op jit(solution)/shard_map/ppermute | solution.py:291

commit v7 on v5

--- a/solution.py
+++ b/solution.py
@@ -21,77 +21,70 @@
     return lax.dot_general(left, right, dims, precision=HIGHEST, preferred_element_type=F32)
 
 
-def pack_kernel(pivots, prior, raw, keep, send, counts, sem):
-    keep[...] = jnp.zeros_like(keep)
-    send[...] = jnp.zeros_like(send)
+def pack_kernel(own, pivots, prior, raw, packed, counts, sem):
+    packed[...] = jnp.zeros_like(packed)
     rows_here = prior.shape[0]
     offset, core = lax.axis_index(AXES) * rows_here, lax.axis_index("core")
-    per_step = pivots.shape[1]
+    half = packed.shape[0] * 8
+    base = (core if own else 1 - core) * half
     chunk = 8
 
     def local(step, pivot):
-        row = pivots[step, pivot] - offset
+        row = pivots[step, base + pivot] - offset
         return row, row.astype(jnp.uint32) < jnp.uint32(rows_here)
 
     def tiles(step):
-        base = 5 * step
+        first = 5 * step
         for t in range(3):
-            yield base + t, prior, 128 * t
+            yield first + t, prior, 128 * t
         for which in range(step + 1):
             for t in range(2):
-                yield base + 3 + 2 * which + t, raw.at[which], 128 * t
+                yield first + 3 + 2 * which + t, raw.at[which], 128 * t
 
     def copy(source, row, column, target):
         return pltpu.make_async_copy(source.at[pl.ds(row, 1), pl.ds(column, 128)], target, sem)
 
-    def start(step, pivot):
-        row, here = local(step, pivot)
+    def start(step, group, line):
+        row, here = local(step, 8 * group + line)
 
         @pl.when(here)
         def _():
             counts[step] += 1
-            half = keep.shape[0]
-            group, line = pivot // 8, pl.ds(lax.rem(pivot, 8), 1)
-            for side, target in ((core, keep), (1 - core, send)):
-
-                @pl.when(group // half == side)
-                def _():
-                    for number, source, column in tiles(step):
-                        copy(source, row, column, target.at[lax.rem(group, half), number, line]).start()
+            for number, source, column in tiles(step):
+                copy(source, row, column, packed.at[group, number, pl.ds(line, 1)]).start()
 
     for step in range(2):
         counts[step] = 0
-
-        for first in range(0, per_step, chunk):
+        for first in range(0, half, chunk):
             found = local(step, first)[1]
             for k in range(1, chunk):
                 found = jnp.logical_or(found, local(step, first + k)[1])
 
             @pl.when(found)
             def _(step=step, first=first):
-                lax.fori_loop(0, chunk, lambda k, _: start(step, first + k), None)
+                lax.fori_loop(0, chunk, lambda k, _: start(step, first // 8, k), None)
 
     for step in range(2):
 
         def finish(_, carry, step=step):
             for _, source, column in tiles(step):
-                copy(source, 0, column, keep.at[0, 0, pl.ds(0, 1)]).wait()
+                copy(source, 0, column, packed.at[0, 0, pl.ds(0, 1)]).wait()
             return carry
 
         lax.fori_loop(0, counts[step], finish, 0)
 
 
-def pack(pivot_rows, prior, raw, groups):
-    shape = pltpu.VMEM((groups, 12) + TILE, F32)
+def pack(own, pivot_rows, prior, raw, groups):
     vmem, smem = pl.BlockSpec(memory_space=pltpu.VMEM), pl.BlockSpec(memory_space=pltpu.SMEM)
     where_it_is = pl.BlockSpec(memory_space=pl.ANY)
     return pl.pallas_call(
-        pack_kernel,
-        out_shape=(shape, shape),
+        functools.partial(pack_kernel, own),
+        out_shape=pltpu.VMEM((groups, 12) + TILE, F32),
         in_specs=[smem, where_it_is, where_it_is],
-        out_specs=(vmem, vmem),
+        out_specs=vmem,
         scratch_shapes=[pltpu.SMEM((2,), jnp.int32), pltpu.SemaphoreType.DMA],
         compiler_params=pltpu.CompilerParams(vmem_limit_bytes=PACK_VMEM_LIMIT),
+        cost_estimate=pl.CostEstimate(flops=0, bytes_accessed=4 * 1024 * 1024, transcendentals=0),
     )(pivot_rows, prior, raw)
 
 
@@ -281,8 +274,8 @@
     in_plane = lax.axis_size(plane)
     swap = [(0, 1), (1, 0)]
 
-    keep, send = pack(pivot_rows, prior, raw, in_plane)
-    total = keep + lax.ppermute(send, "core", swap)
+    came = lax.ppermute(pack(False, pivot_rows, prior, raw, in_plane), "core", swap)
+    total = pack(True, pivot_rows, prior, raw, in_plane) + came
     total = jnp.sum(lax.all_to_all(total, plane, 0, 0), axis=0)
     for groups in ([[4 * run + k for k in range(4)] for run in range(4)], [[4 * run + k for run in range(4)] for k in range(4)]):
         copies = jnp.broadcast_to(total, (4,) + total.shape)

time: 106 us -> 105 us (level)
  waiting for transfers between devices: 3.6 us -> 1.94 us
  Pallas kernels: 17.7 us -> 19 us
    ppermute x1, waiting for transfers between devices: 1.89 us -> 0.23 us  [body(): lax.ppermute(pack(False, pivot_rows, prior, raw, in_plane), 'core', swap)]
    pallas_call x1 -> x2, Pallas kernels: 2 us -> 3.29 us  [pack(): pl.pallas_call(functools.partial(pack_kernel, own), out_shape=pltpu.VMEM(...]
  transfers between devices with their start and end apart: 2 -> 2, of which waited for: 2 -> 2; matrix products, arithmetic and copies ran while one was open for 0% -> 0% of each run, Pallas kernels for 0% -> 2%
where the time goes in v7:
time: 105 us
  blocking collectives  67 us (64%)
  Pallas kernels  19 us (18%)
  starting transfers between devices  16.2 us (15%)
  waiting for transfers between devices  1.94 us (2%)
    all_to_all x2, blocking collectives, body(): lax.all_to_all(copies, line, 0, 0, axis_index_groups=groups)  36.6 us
    all_to_all x1, blocking collectives, body(): total = jnp.sum(lax.all_to_all(total, plane, 0, 0), axis=0)  16.7 us
    pallas_call x1, Pallas kernels, steps(): pl.pallas_call(steps_kernel, out_shape=jax.ShapeDtypeStruct(raw.shape, F3...  15.7 us
    all_to_all x1, blocking collectives, body(): lax.all_to_all(jnp.broadcast_to(total, (in_plane,) + total.shape), plane,...  13.6 us
    ppermute x1, starting transfers between devices, body(): lax.ppermute(pack(False, pivot_rows, prior, raw, in_plane), 'core', swap)  9.34 us
    ppermute x1, starting transfers between devices, body(): other = lax.ppermute(mine, 'core', swap)  6.85 us
    pallas_call x2, Pallas kernels, pack(): pl.pallas_call(functools.partial(pack_kernel, own), out_shape=pltpu.VMEM(...  3.29 us
  transfers between devices with their start and end apart: 2, of which 2 were waited for; matrix products, arithmetic and copies ran while one was open for 0% of the time, Pallas kernels for 2%

profile of v7, /device:TPU:1, one launch (start us, length us, event | category | flops | bytes accessed | tf_op | source)
XLA Modules:
  0.0 104.6 jit_solution(14238314795121997364)
XLA Ops:
  0.0 1.6 %shard_map.38 = f32[16,12,8,128]{3,2,1,0:T(8,128)S(1)} custom-call(s32[2,256]{1,0:T(2,128)} %pivots.3, f32[896,384]{1,0:T(8,128)} %prior.5, f32[2,896,256]{2,1,0:T(8,128)} %raw.5), custom_call_target="tpu_custom_call" | custom-call | bytes 4194304 | tf_op jit(solution)/shard_map/pallas_call | solution.py:80
  1.7 9.3 %collective-permute-start = (f32[16,12,8,128]{3,2,1,0:T(8,128)S(1)}, f32[16,12,8,128]{3,2,1,0:T(8,128)S(1)}, u32[]{:S(2)}, u32[]{:S(2)}) collective-permute-start(f32[16,12,8,128]{3,2,1,0:T(8,128)S(1)} %shard_map.38), channel_id=1, source_target_pairs={{0,8},{8,0},{1,9},{9,1},{2,10},{10,2},{3,11},{11,3},{4,12},{12,4},... | collective-permute-start | bytes 2359304 | tf_op jit(solution)/shard_map/ppermute | solution.py:277
  11.0 1.6 %shard_map.37 = f32[16,12,8,128]{3,2,1,0:T(8,128)S(1)} custom-call(s32[2,256]{1,0:T(2,128)} %pivots.3, f32[896,384]{1,0:T(8,128)} %prior.5, f32[2,896,256]{2,1,0:T(8,128)} %raw.5), custom_call_target="tpu_custom_call" | custom-call | bytes 4194304 | tf_op jit(solution)/shard_map/pallas_call | solution.py:80
  12.7 0.2 collective-permute-done
  12.9 0.1 add.3
  13.0 16.7 %all_to_all.20 = f32[16,12,8,128]{3,2,1,0:T(8,128)S(1)} all-to-all(f32[16,12,8,128]{3,2,1,0:T(8,128)S(1)} %add.3), channel_id=1, replica_groups=mesh['z_hi'=2,'y'=4,'x'=4,'core'=2,'z_lo'=8] {'y','x'}, dimensions={0} | all-to-all | bytes 1572864 | tf_op jit(solution)/shard_map/all_to_all | solution.py:279
  29.7 9.1 %all_to_all.21 = f32[4,12,8,128]{3,2,1,0:T(8,128)S(1)} all-to-all(f32[4,12,8,128]{3,2,1,0:T(8,128)S(1)} %broadcast_in_dim.9), channel_id=1, replica_groups={{0,1,2,3},{4,5,6,7},{256,257,258,259},{260,261,262,263},{8,9,10,11},{12..., dimensions={0} | all-to-all | bytes 393216 | tf_op jit(solution)/shard_map/all_to_all | solution.py:282
  38.8 0.0 copy-start
  38.8 0.0 copy-start.1
  38.8 27.6 %all_to_all.22 = f32[4,12,8,128]{3,2,1,0:T(8,128)S(1)} all-to-all(f32[4,12,8,128]{3,2,1,0:T(8,128)S(1)} %broadcast_in_dim.10), channel_id=1, replica_groups={{0,4,256,260},{1,5,257,261},{2,6,258,262},{3,7,259,263},{8,12,264,268},..., dimensions={0} | all-to-all | bytes 393216 | tf_op jit(solution)/shard_map/all_to_all | solution.py:282
  66.4 0.1 broadcast_in_dim.11
  66.5 13.6 %all_to_all.23.mine = f32[16,12,8,128]{3,2,1,0:T(8,128)S(1)} all-to-all(f32[16,12,8,128]{3,2,1,0:T(8,128)S(1)} %broadcast_in_dim.11), channel_id=1, replica_groups=mesh['z_hi'=2,'y'=4,'x'=4,'core'=2,'z_lo'=8] {'y','x'}, dimensions={0} | all-to-all | bytes 1572864 | tf_op jit(solution)/shard_map/all_to_all | solution.py:283
  80.1 6.8 %collective-permute-start.1 = (f32[16,12,8,128]{3,2,1,0:T(8,128)S(1)}, f32[16,12,8,128]{3,2,1,0:T(8,128)S(1)}, u32[]{:S(2)}, u32[]{:S(2)}) collective-permute-start(f32[16,12,8,128]{3,2,1,0:T(8,128)S(1)} %all_to_all.23.mine), channel_id=1, source_target_pairs={{0,8},{8,0},{1,9},{9,1},{2,10},{10,2},{3,11},{11,3},{4,12},{12,4},... | collective-permute-start | bytes 2359304 | tf_op jit(solution)/shard_map/ppermute | solution.py:284
  87.0 1.7 %collective-permute-done.1.other = f32[16,12,8,128]{3,2,1,0:T(8,128)S(1)} collective-permute-done((f32[16,12,8,128]{3,2,1,0:T(8,128)S(1)}, f32[16,12,8,128]{3,2,1,0:T(8,128)S(1)}, u32[]{:S(2)}, u32[]{:S(2)}) %collective-permute-start.1) | collective-permute-done | bytes 786464 | tf_op jit(solution)/shard_map/ppermute | solution.py:284
  88.7 0.0 copy-done
  88.7 0.0 copy-done.1
  88.7 15.7 %shard_map.39 = f32[2,896,256]{2,1,0:T(8,128)} custom-call(f32[16,12,8,128]{3,2,1,0:T(8,128)S(1)} %all_to_all.23.mine, f32[16,12,8,128]{3,2,1,0:T(8,128)S(1)} %collective-permute-done.1.other, f32[896,384]{1,0:T(8,128)S(1)} %copy-done.1, f32[2,896,256]{2,1,0:T(8,128)S(1)} %copy-done), custom_call_target="tpu_custom_call" | custom-call | tf_op jit(solution)/shard_map/pallas_call | solution.py:258
  (5 shorter events, 0.1 us)
Async XLA Ops:
  1.7 11.2 %collective-permute-start = (f32[16,12,8,128]{3,2,1,0:T(8,128)S(1)}, f32[16,12,8,128]{3,2,1,0:T(8,128)S(1)}, u32[]{:S(2)}, u32[]{:S(2)}) collective-permute-start(f32[16,12,8,128]{3,2,1,0:T(8,128)S(1)} %shard_map.38), channel_id=1, source_target_pairs={{0,8},{8,0},{1,9},{9,1},{2,10},{10,2},{3,11},{11,3},{4,12},{12,4},... | collective-permute-start | bytes 2359304 | tf_op jit(solution)/shard_map/ppermute | solution.py:277
  38.8 49.9 %copy-start = (f32[2,896,256]{2,1,0:T(8,128)S(1)}, f32[2,896,256]{2,1,0:T(8,128)}, u32[]{:S(2)}) copy-start(f32[2,896,256]{2,1,0:T(8,128)} %raw.5) | copy-start | bytes 5505028
  38.8 49.9 %copy-start.1 = (f32[896,384]{1,0:T(8,128)S(1)}, f32[896,384]{1,0:T(8,128)}, u32[]{:S(2)}) copy-start(f32[896,384]{1,0:T(8,128)} %prior.5) | copy-start | bytes 4128772
  80.1 8.6 %collective-permute-start.1 = (f32[16,12,8,128]{3,2,1,0:T(8,128)S(1)}, f32[16,12,8,128]{3,2,1,0:T(8,128)S(1)}, u32[]{:S(2)}, u32[]{:S(2)}) collective-permute-start(f32[16,12,8,128]{3,2,1,0:T(8,128)S(1)} %all_to_all.23.mine), channel_id=1, source_target_pairs={{0,8},{8,0},{1,9},{9,1},{2,10},{10,2},{3,11},{11,3},{4,12},{12,4},... | collective-permute-start | bytes 2359304 | tf_op jit(solution)/shard_map/ppermute | solution.py:284
